TPU v7x, 128 devices: a whole 4x4x4 slice. The times are simulated.
128 devices in a mesh: rows: 8 (over y, core), seq: 16 (over z, x).
Axes of the slice: x: 4, y: 4, z: 4, core: 2. Of those that a mesh axis runs over, the one named last changes fastest.
Arguments:
- block_input: bfloat16 [8, 2048, 768], P('rows', 'seq'), may hold values from -6 to 6
- offsets: int32 [8, 8], P('rows'), may hold values from 0 to 2047, as said below
- ln1_gain: bfloat16 [768], replicated, may hold values from 0.099609375 to 1.8984375
- ln1_bias: bfloat16 [768], replicated, may hold values from -3 to 3
- w_qkv: bfloat16 [768, 2304], replicated, may hold values from -0.21875 to 0.21875
- bias_query: bfloat16 [768], replicated, may hold values from -3 to 3
- bias_value: bfloat16 [768], replicated, may hold values from -3 to 3
- w_out: bfloat16 [768, 768], replicated, may hold values from -1.25 to 1.25
- bias_out: bfloat16 [768], replicated, may hold values from -3 to 3
- ln2_gain: bfloat16 [768], replicated, may hold values from 0.099609375 to 1.8984375
- ln2_bias: bfloat16 [768], replicated, may hold values from -3 to 3
- w_up: bfloat16 [768, 3072], replicated, may hold values from -0.21875 to 0.21875
- bias_up: bfloat16 [3072], replicated, may hold values from -3 to 3
- w_down: bfloat16 [3072, 768], replicated, may hold values from -0.109375 to 0.109375
- bias_down: bfloat16 [768], replicated, may hold values from -3 to 3
- cotangent: bfloat16 [8, 2048, 768], P('rows', 'seq'), may hold values from -6 to 6
Outputs:
- block_output: bfloat16 [8, 2048, 768], P('rows', 'seq')
- input_grad: bfloat16 [8, 2048, 768], P('rows', 'seq')
- grad_ln1_gain: float32 [768], replicated
- grad_ln1_bias: float32 [768], replicated
- grad_w_qkv: float32 [768, 2304], replicated
- grad_bias_query: float32 [768], replicated
- grad_bias_value: float32 [768], replicated
- grad_w_out: float32 [768, 768], replicated
- grad_bias_out: float32 [768], replicated
- grad_ln2_gain: float32 [768], replicated
- grad_ln2_bias: float32 [768], replicated
- grad_w_up: float32 [768, 3072], replicated
- grad_bias_up: float32 [3072], replicated
- grad_w_down: float32 [3072, 768], replicated
- grad_bias_down: float32 [768], replicated
Inputs may be any that keep to these rules, and one draw needn't show every extreme that they name: Each row's offsets start at 0 and rise strictly; segment j of a row covers positions offsets[j] to offsets[j + 1] - 1, the last one to position 2047.
All inputs are finite; a program needn't handle non-finite values.
Results may differ from a plain program's by a relative error of at most 0.011.
Values may be sent and summed in bfloat16 or wider, within the bound.
A program may use at most 192 MiB of HBM per device.

v0:
```python
import jax
import jax.numpy as jnp
from jax import lax
from jax.sharding import PartitionSpec as P

H = 16
QBLOCK = 512


EPSILON = 1e-05
NEGATIVE = -1e30


def layer_norm(values, gain_vec, bias_vec):
    center = values - jnp.mean(values, axis=-1, keepdims=True)
    spread = jnp.mean(center * center, axis=-1, keepdims=True)
    return center * lax.rsqrt(spread + EPSILON) * gain_vec + bias_vec


def segment_ids(offsets, length):
    positions = jnp.arange(length, dtype=jnp.int32)
    hits = (offsets[:, None, :] <= positions[None, :, None]).astype(jnp.int32)
    return jnp.sum(hits, axis=-1) - 1


def project(left, right):
    return jnp.einsum("rpd,de->rpe", left, right, preferred_element_type=jnp.float32)


def project_back(left, right):
    return jnp.einsum("rpe,de->rpd", left, right, preferred_element_type=jnp.float32)


def weight_grad(left, right):
    return jnp.einsum("rpd,rpe->de", left, right, preferred_element_type=jnp.float32)


def token_sum(values):
    return jnp.sum(values.astype(jnp.float32), axis=(0, 1))


def masked_scores(query_part, key_heads, seg_part, segments, first_row, score_scale):
    rows_here = query_part.shape[0]
    raw = (
        jnp.einsum("qhd,khd->hqk", query_part, key_heads, preferred_element_type=jnp.float32)
        * score_scale
    )
    query_place = first_row + jnp.arange(rows_here, dtype=jnp.int32)
    key_place = jnp.arange(key_heads.shape[0], dtype=jnp.int32)
    allowed = (seg_part[:, None] == segments[None, :]) & (
        key_place[None, :] <= query_place[:, None]
    )
    return jnp.where(allowed[None], raw, NEGATIVE)


def attend_forward(queries, key_rows, value_rows, segments_all, head_size, query_block):
    row_count, length, local_width = queries.shape
    local_heads = local_width // head_size
    block_count = length // query_block
    score_scale = head_size ** (-0.5)

    def one_row(packed):
        query_row, key_row, value_row, segments = packed
        key_heads = key_row.reshape(length, local_heads, head_size)
        value_heads = value_row.reshape(length, local_heads, head_size)

        def one_block(block_index):
            first_row = block_index * query_block
            query_part = lax.dynamic_slice_in_dim(query_row, first_row, query_block, 0).reshape(
                query_block, local_heads, head_size
            )
            seg_part = lax.dynamic_slice_in_dim(segments, first_row, query_block, 0)
            scores = masked_scores(
                query_part, key_heads, seg_part, segments, first_row, score_scale
            )
            highest = jnp.max(scores, axis=-1, keepdims=True)
            exp_scores = jnp.exp(scores - highest)
            totals = jnp.sum(exp_scores, axis=-1, keepdims=True)
            probs_low = (exp_scores / totals).astype(jnp.bfloat16)
            attended = jnp.einsum(
                "hqk,khd->qhd", probs_low, value_heads, preferred_element_type=jnp.float32
            )
            return (
                attended.reshape(query_block, local_width).astype(jnp.bfloat16),
                (highest + jnp.log(totals))[..., 0],
            )

        attended, log_sums = lax.map(one_block, jnp.arange(block_count, dtype=jnp.int32))
        return (
            attended.reshape(length, local_width),
            jnp.transpose(log_sums, (1, 0, 2)).reshape(local_heads, length),
        )

    return lax.map(one_row, (queries, key_rows, value_rows, segments_all))


def attend_backward(
    queries, key_rows, value_rows, grad_rows, log_sums, segments_all, head_size, query_block
):
    row_count, length, local_width = queries.shape
    local_heads = local_width // head_size
    block_count = length // query_block
    score_scale = head_size ** (-0.5)

    def one_row(packed):
        query_row, key_row, value_row, grad_row, log_row, segments = packed
        key_heads = key_row.reshape(length, local_heads, head_size)
        value_heads = value_row.reshape(length, local_heads, head_size)

        def one_block(carry, block_index):
            key_acc, value_acc = carry
            first_row = block_index * query_block
            query_part = lax.dynamic_slice_in_dim(query_row, first_row, query_block, 0).reshape(
                query_block, local_heads, head_size
            )
            grad_part = lax.dynamic_slice_in_dim(grad_row, first_row, query_block, 0).reshape(
                query_block, local_heads, head_size
            )
            log_part = lax.dynamic_slice_in_dim(log_row, first_row, query_block, 1)
            seg_part = lax.dynamic_slice_in_dim(segments, first_row, query_block, 0)
            scores = masked_scores(
                query_part, key_heads, seg_part, segments, first_row, score_scale
            )
            probs = jnp.exp(scores - log_part[..., None])
            grad_probs = jnp.einsum(
                "qhd,khd->hqk", grad_part, value_heads, preferred_element_type=jnp.float32
            )
            inner = jnp.sum(probs * grad_probs, axis=-1, keepdims=True)
            grad_scores = (probs * (grad_probs - inner)).astype(jnp.bfloat16)
            probs_low = probs.astype(jnp.bfloat16)
            grad_query = (
                jnp.einsum(
                    "hqk,khd->qhd", grad_scores, key_heads, preferred_element_type=jnp.float32
                )
                * score_scale
            )
            key_acc = (
                key_acc
                + jnp.einsum(
                    "hqk,qhd->khd", grad_scores, query_part, preferred_element_type=jnp.float32
                )
                * score_scale
            )
            value_acc = value_acc + jnp.einsum(
                "hqk,qhd->khd", probs_low, grad_part, preferred_element_type=jnp.float32
            )
            return (
                (key_acc, value_acc),
                grad_query.reshape(query_block, local_width).astype(jnp.bfloat16),
            )

        zeros = jnp.zeros((length, local_heads, head_size), jnp.float32)
        (key_acc, value_acc), grad_queries = lax.scan(
            one_block, (zeros, zeros), jnp.arange(block_count, dtype=jnp.int32)
        )
        return (
            grad_queries.reshape(length, local_width),
            key_acc.reshape(length, local_width).astype(jnp.bfloat16),
            value_acc.reshape(length, local_width).astype(jnp.bfloat16),
        )

    return lax.map(one_row, (queries, key_rows, value_rows, grad_rows, log_sums, segments_all))


def gelu_tanh(values):
    return jax.nn.gelu(values, approximate=True)


def local(
    block_input,
    offsets,
    ln1_gain,
    ln1_bias,
    w_qkv,
    bias_query,
    bias_value,
    w_out,
    bias_out,
    ln2_gain,
    ln2_bias,
    w_up,
    bias_up,
    w_down,
    bias_down,
    cotangent,
):
    width = block_input.shape[2]
    full_length = block_input.shape[1] * lax.axis_size("seq")
    head_size = width // H
    segments = segment_ids(offsets, full_length)
    gain_one = ln1_gain.astype(jnp.float32)
    shift_one = ln1_bias.astype(jnp.float32)
    gain_two = ln2_gain.astype(jnp.float32)
    shift_two = ln2_bias.astype(jnp.float32)
    start_input = block_input.astype(jnp.float32)
    h_one = layer_norm(start_input, gain_one, shift_one).astype(jnp.bfloat16)
    projected = project(h_one, w_qkv)
    queries = (projected[..., 0:width] + bias_query.astype(jnp.float32)).astype(jnp.bfloat16)
    key_rows = projected[..., width : 2 * width].astype(jnp.bfloat16)
    value_rows = (projected[..., 2 * width : 3 * width] + bias_value.astype(jnp.float32)).astype(
        jnp.bfloat16
    )
    query_heads, key_heads, value_heads = (
        lax.all_to_all(queries, "seq", split_axis=2, concat_axis=1, tiled=True),
        lax.all_to_all(key_rows, "seq", split_axis=2, concat_axis=1, tiled=True),
        lax.all_to_all(value_rows, "seq", split_axis=2, concat_axis=1, tiled=True),
    )
    attended_heads, log_sums = attend_forward(
        query_heads, key_heads, value_heads, segments, head_size, QBLOCK
    )
    attended = lax.all_to_all(attended_heads, "seq", split_axis=1, concat_axis=2, tiled=True)
    resid = start_input + project(attended, w_out) + bias_out.astype(jnp.float32)
    h_two = layer_norm(resid, gain_two, shift_two).astype(jnp.bfloat16)
    pre_act = project(h_two, w_up) + bias_up.astype(jnp.float32)
    act_low = gelu_tanh(pre_act).astype(jnp.bfloat16)
    block_output = (resid + project(act_low, w_down) + bias_down.astype(jnp.float32)).astype(
        jnp.bfloat16
    )
    grad_w_down = weight_grad(act_low, cotangent)
    grad_bias_down = token_sum(cotangent)
    grad_act = project_back(cotangent, w_down)
    unused_value, gelu_back = jax.vjp(gelu_tanh, pre_act)
    grad_pre = gelu_back(grad_act)[0].astype(jnp.bfloat16)
    grad_w_up = weight_grad(h_two, grad_pre)
    grad_bias_up = token_sum(grad_pre)
    grad_h_two = project_back(grad_pre, w_up)
    unused_norm, norm_two_back = jax.vjp(layer_norm, resid, gain_two, shift_two)
    resid_part, grad_ln2_gain, grad_ln2_bias = norm_two_back(grad_h_two)
    grad_resid = cotangent.astype(jnp.float32) + resid_part
    grad_branch = grad_resid.astype(jnp.bfloat16)
    grad_w_out = weight_grad(attended, grad_branch)
    grad_bias_out = token_sum(grad_branch)
    grad_attended = project_back(grad_branch, w_out).astype(jnp.bfloat16)
    grad_attended_heads = lax.all_to_all(
        grad_attended, "seq", split_axis=2, concat_axis=1, tiled=True
    )
    grad_query_heads, grad_key_heads, grad_value_heads = attend_backward(
        query_heads,
        key_heads,
        value_heads,
        grad_attended_heads,
        log_sums,
        segments,
        head_size,
        QBLOCK,
    )
    grad_queries, grad_keys, grad_values = (
        lax.all_to_all(grad_query_heads, "seq", split_axis=1, concat_axis=2, tiled=True),
        lax.all_to_all(grad_key_heads, "seq", split_axis=1, concat_axis=2, tiled=True),
        lax.all_to_all(grad_value_heads, "seq", split_axis=1, concat_axis=2, tiled=True),
    )
    grad_projected = jnp.concatenate([grad_queries, grad_keys, grad_values], axis=-1)
    grad_w_qkv = weight_grad(h_one, grad_projected)
    grad_bias_query = token_sum(grad_queries)
    grad_bias_value = token_sum(grad_values)
    grad_h_one = project_back(grad_projected, w_qkv)
    unused_first, norm_one_back = jax.vjp(layer_norm, start_input, gain_one, shift_one)
    input_part, grad_ln1_gain, grad_ln1_bias = norm_one_back(grad_h_one)
    input_grad = (grad_resid + input_part).astype(jnp.bfloat16)
    summed = lax.psum(
        (
            grad_ln1_gain,
            grad_ln1_bias,
            grad_w_qkv,
            grad_bias_query,
            grad_bias_value,
            grad_w_out,
            grad_bias_out,
            grad_ln2_gain,
            grad_ln2_bias,
            grad_w_up,
            grad_bias_up,
            grad_w_down,
            grad_bias_down,
        ),
        ("rows", "seq"),
    )
    return (
        block_output,
        input_grad,
        summed[0],
        summed[1],
        summed[2],
        summed[3],
        summed[4],
        summed[5],
        summed[6],
        summed[7],
        summed[8],
        summed[9],
        summed[10],
        summed[11],
        summed[12],
    )


def solution(mesh):
    placed = (
        P("rows", "seq", None),
        P("rows", None),
        P(),
        P(),
        P(),
        P(),
        P(),
        P(),
        P(),
        P(),
        P(),
        P(),
        P(),
        P(),
        P(),
        P("rows", "seq", None),
    )
    return jax.shard_map(
        local,
        mesh=mesh,
        in_specs=placed,
        out_specs=(
            P("rows", "seq", None),
            P("rows", "seq", None),
            P(),
            P(),
            P(),
            P(),
            P(),
            P(),
            P(),
            P(),
            P(),
            P(),
            P(),
            P(),
            P(),
        ),
        check_vma=False,
    )
```

profile of v0, /device:TPU:1, one launch (start us, length us, event | category | flops | bytes accessed | tf_op | source)
XLA Modules:
  0.0 644.1 jit_solution(9212779496981082066)
XLA Ops:
  18.2 3.4 reduce.27
  23.3 8.6 %all-to-all-start.2 = ((bf16[16,2,3072]{2,1,0:T(2,128)(2,1)}), bf16[16,2,3072]{2,1,0:T(2,128)(2,1)}, u32[]{:S(2)}, u32[]{:S(2)}) async-start(bf16[16,2,3072]{2,1,0:T(2,128)(2,1)} %reshape.520), calls=%async_computation.2 | async-start | bytes 393216 | tf_op jit(solution)/shard_map/all_to_all | solution.py:206
  35.5 3.4 reduce.26
  40.6 6.7 %all-to-all-start.1 = ((bf16[16,2,3072]{2,1,0:T(2,128)(2,1)}), bf16[16,2,3072]{2,1,0:T(2,128)(2,1)}, u32[]{:S(2)}, u32[]{:S(2)}) async-start(bf16[16,2,3072]{2,1,0:T(2,128)(2,1)} %reshape.518), calls=%async_computation.1 | async-start | bytes 393216 | tf_op jit(solution)/shard_map/all_to_all | solution.py:205
  49.2 3.4 reduce.25
  54.9 6.8 %all-to-all-start = ((bf16[16,2,3072]{2,1,0:T(2,128)(2,1)}), bf16[16,2,3072]{2,1,0:T(2,128)(2,1)}, u32[]{:S(2)}, u32[]{:S(2)}) async-start(bf16[16,2,3072]{2,1,0:T(2,128)(2,1)} %reshape.516), calls=%async_computation | async-start | bytes 393216 | tf_op jit(solution)/shard_map/all_to_all | solution.py:204
  80.9 29.9 %while.47 = (s32[]{:T(128)}, bf16[4,512,48]{1,2,0:T(8,128)(2,1)}, f32[4,1,512]{2,1,0:T(1,128)}, s32[4]{0:T(128)}, s32[2048]{0:T(1024)S(1)}, /*index=5*/bf16[2048...) while((s32[]{:T(128)}, bf16[4,512,48]{1,2,0:T(8,128)(2,1)}, ...), condition=%wide.region_6.7_spmd, body=%wide.region_3.6_spmd.sunk | while | flops 212885504 | bytes 13981927 | solution.py:88
  112.7 4.1 reshape.514
  116.7 13.4 %reduce.28 = bf16[2048,48]{1,0:T(8,128)(2,1)} reduce(bf16[2048,1,48]{2,1,0:T(2,128)(2,1)} %bitcast.257, bf16[]{:T(256)} %broadcast.314), dimensions={1}, to_apply=%bitcast.184.reduce_sub_computation | reduce | bytes 393218
  130.1 2.5 reshape.522
  132.6 7.0 %all-to-all-start.3 = ((bf16[16,2,3072]{2,1,0:T(2,128)(2,1)}), bf16[16,2,3072]{2,1,0:T(2,128)(2,1)}, u32[]{:S(2)}, u32[]{:S(2)}) async-start(bf16[16,2,3072]{2,1,0:T(2,128)(2,1)} %reshape.522), calls=%async_computation.3 | async-start | bytes 393216 | tf_op jit(solution)/shard_map/all_to_all | solution.py:211
  143.6 3.3 all-to-all-done.3
  146.9 3.5 reshape.523
  150.3 3.4 copy.171
  156.9 3.3 convolution_add_fusion
  160.2 5.5 convert_reduce_fusion
  173.6 3.4 reduce.29
  178.7 4.4 all-to-all-start.4
  183.1 6.7 %fusion.66 = f32[3072,768]{1,0:T(8,128)} fusion(bf16[1,128,768]{2,1,0:T(8,128)(2,1)} %param.35, f32[128,3072]{1,0:T(8,128)} %copy-done.6), kind=kOutput, calls=%fused_computation.109 | convolution fusion | flops 607518720 | bytes 11206656 | tf_op jit(solution)/shard_map/rpd,rpe->de/dot_general | solution.py:35
  197.4 48.3 %while.48 = (s32[]{:T(128)}, f32[2048,1,48]{0,2,1:T(8,128)}, f32[2048,1,48]{0,2,1:T(8,128)}, bf16[4,512,48]{1,2,0:T(8,128)(2,1)}, s32[4]{0:T(128)}, /*index=5*/b...) while((s32[]{:T(128)}, f32[2048,1,48]{0,2,1:T(8,128)}, ...), condition=%wide.region_13.14_spmd.clone, body=%wide.region_11.13_spmd.clone.sunk | while | flops 516440064 | bytes 42119612 | solution.py:153
  247.6 4.1 reshape.515
  251.7 13.8 %reduce.32 = bf16[2048,48]{1,0:T(8,128)(2,1)} reduce(bf16[2048,1,48]{2,1,0:T(2,128)(2,1)} %bitcast.258, bf16[]{:T(256)} %broadcast.314), dimensions={1}, to_apply=%bitcast.192.reduce_sub_computation | reduce | bytes 393218
  268.0 6.4 all-to-all-start.5
  276.4 3.3 copy.184
  279.7 13.4 %reduce.30 = bf16[2048,48]{1,0:T(8,128)(2,1)} reduce(bf16[2048,1,48]{2,1,0:T(2,128)(2,1)} %bitcast.259, bf16[]{:T(256)} %broadcast.314), dimensions={1}, to_apply=%bitcast.188.reduce_sub_computation | reduce | bytes 393218
  293.1 2.5 reshape.526
  295.6 7.0 %all-to-all-start.7 = ((bf16[16,2,3072]{2,1,0:T(2,128)(2,1)}), bf16[16,2,3072]{2,1,0:T(2,128)(2,1)}, u32[]{:S(2)}, u32[]{:S(2)}) async-start(bf16[16,2,3072]{2,1,0:T(2,128)(2,1)} %reshape.526), calls=%async_computation.7 | async-start | bytes 393216 | tf_op jit(solution)/shard_map/all_to_all | solution.py:250
  302.6 6.5 %fusion.79 = f32[768,3072]{1,0:T(8,128)} fusion(bf16[128,3072]{1,0:T(8,128)(2,1)} %copy-done.13, f32[1,128,768]{2,1,0:T(8,128)} %copy-done.1, f32[768]{0:T(1024)S(1)} %convert_element_type.195, f32[768]{0:T(1024)S(1)} %convert_element_type.194, f32[128]{0:T(128)} %copy-done.34, f32[128]{0:T(128)} %copy-done.26), kind=kOutput, calls=%fused_computation.131 | convolution fusion | flops 604471296 | bytes 10624000 | tf_op jit(solution)/shard_map/rpd,rpe->de/dot_general | solution.py:35
  309.1 3.3 copy.181
  312.5 13.4 %reduce.31 = bf16[2048,48]{1,0:T(8,128)(2,1)} reduce(bf16[2048,1,48]{2,1,0:T(2,128)(2,1)} %bitcast.256, bf16[]{:T(256)} %broadcast.314), dimensions={1}, to_apply=%bitcast.190.reduce_sub_computation | reduce | bytes 393218
  325.8 2.5 reshape.528
  328.3 6.8 %all-to-all-start.6 = ((bf16[16,2,3072]{2,1,0:T(2,128)(2,1)}), bf16[16,2,3072]{2,1,0:T(2,128)(2,1)}, u32[]{:S(2)}, u32[]{:S(2)}) async-start(bf16[16,2,3072]{2,1,0:T(2,128)(2,1)} %reshape.528), calls=%async_computation.6 | async-start | bytes 393216 | tf_op jit(solution)/shard_map/all_to_all | solution.py:249
  335.2 2.9 fusion.63
  338.0 3.7 reshape.531
  341.7 3.4 copy.179
  347.5 3.5 reshape.527
  351.0 3.4 copy.185
  356.7 3.5 reshape.529
  360.2 3.4 copy.182
  365.3 5.3 fusion.59
  372.9 4.6 fusion.41
  383.0 3.8 fusion.53
  391.1 2.9 convert_reduce_fusion.2
  393.9 72.1 %all-reduce = (f32[768]{0:T(1024)}, f32[768]{0:T(1024)}, f32[768]{0:T(1024)}, f32[768]{0:T(1024)}, f32[768]{0:T(1024)}, /*index=5*/f32[768]{0:T(1024)}, f32[768]{0:T(1024)}, f32[3072]{0:T(1024)}, f32[768]{0:T(1024)}) all-reduce(f32[768]{0:T(1024)} %get-tuple-element.325, ...), channel_id=1, replica_groups=mesh['rows'=8,'seq'=16] {'rows','seq'}, use_global_device_ids=true, to_apply=%region_17.18 | all-reduce | flops 9216 | bytes 73728 | tf_op jit(solution)/shard_map/psum | solution.py:260
  466.1 149.8 %all-reduce.4.cloned.1.call-done = (f32[768,2304]{1,0:T(8,128)}, f32[768,768]{1,0:T(8,128)}, f32[768,3072]{1,0:T(8,128)}, f32[3072,768]{1,0:T(8,128)}) async-done(((f32[768,2304]{1,0:T(8,128)}, f32[768,768]{1,0:T(8,128)}, f32[768,3072]{1,0:T(8,128)}, f32[3072,768]{1,0:T(8,128)}), (f32[768,2304]{1,0:T(8,128)}, f32[768,768]{1,0:T(8,128)}, f32[768,3072]{1,0:T(8,128)}, ...) | async-done | bytes 28311568 | tf_op jit(solution)/shard_map/psum | solution.py:260
  615.9 6.6 %copy.233 = f32[768,2304]{1,0:T(8,128)} copy(f32[768,2304]{1,0:T(8,128)} %get-tuple-element.608) | data formatting | bytes 14155776
  623.9 9.3 %copy.235 = f32[768,3072]{1,0:T(8,128)} copy(f32[768,3072]{1,0:T(8,128)} %get-tuple-element.615) | data formatting | bytes 18874368
  633.2 3.7 copy.236
  (301 shorter events, 166.0 us)
Async XLA Ops:
  7.2 5.1 copy-start
  8.4 5.5 copy-start.30
  9.5 2.1 copy-start.37
  9.5 4.4 copy-start.27
  23.3 31.0 %copy-start.38 = (s32[1,8]{1,0:T(1,128)S(1)}, s32[1,8]{1,0:T(1,128)}, u32[]{:S(2)}) copy-start(s32[1,8]{1,0:T(1,128)} %param.21) | copy-start | bytes 100
  23.3 17.3 %all-to-all-start.2 = ((bf16[16,2,3072]{2,1,0:T(2,128)(2,1)}), bf16[16,2,3072]{2,1,0:T(2,128)(2,1)}, u32[]{:S(2)}, u32[]{:S(2)}) async-start(bf16[16,2,3072]{2,1,0:T(2,128)(2,1)} %reshape.520), calls=%async_computation.2 | async-start | bytes 393216 | tf_op jit(solution)/shard_map/all_to_all | solution.py:206
  40.6 14.4 %all-to-all-start.1 = ((bf16[16,2,3072]{2,1,0:T(2,128)(2,1)}), bf16[16,2,3072]{2,1,0:T(2,128)(2,1)}, u32[]{:S(2)}, u32[]{:S(2)}) async-start(bf16[16,2,3072]{2,1,0:T(2,128)(2,1)} %reshape.518), calls=%async_computation.1 | async-start | bytes 393216 | tf_op jit(solution)/shard_map/all_to_all | solution.py:205
  54.9 18.9 %all-to-all-start = ((bf16[16,2,3072]{2,1,0:T(2,128)(2,1)}), bf16[16,2,3072]{2,1,0:T(2,128)(2,1)}, u32[]{:S(2)}, u32[]{:S(2)}) async-start(bf16[16,2,3072]{2,1,0:T(2,128)(2,1)} %reshape.516), calls=%async_computation | async-start | bytes 393216 | tf_op jit(solution)/shard_map/all_to_all | solution.py:204
  110.7 21.9 %copy-start.23 = (s32[2048]{0:T(1024)}, s32[2048]{0:T(1024)S(1)}, u32[]{:S(2)}) copy-start(s32[2048]{0:T(1024)S(1)} %get-tuple-element.656) | copy-start | bytes 24580
  132.6 14.3 %all-to-all-start.3 = ((bf16[16,2,3072]{2,1,0:T(2,128)(2,1)}), bf16[16,2,3072]{2,1,0:T(2,128)(2,1)}, u32[]{:S(2)}, u32[]{:S(2)}) async-start(bf16[16,2,3072]{2,1,0:T(2,128)(2,1)} %reshape.522), calls=%async_computation.3 | async-start | bytes 393216 | tf_op jit(solution)/shard_map/all_to_all | solution.py:211
  153.7 3.1 copy-start.25
  154.7 2.1 copy-start.20
  156.6 11.4 %copy-start.1 = (f32[1,128,768]{2,1,0:T(8,128)}, f32[1,128,768]{2,1,0:T(8,128)S(1)}, u32[]{:S(2)}) copy-start(f32[1,128,768]{2,1,0:T(8,128)S(1)} %get-tuple-element.391) | copy-start | bytes 1179652
  156.6 11.4 %copy-start.26 = (f32[128]{0:T(128)}, f32[128]{0:T(128)S(1)}, u32[]{:S(2)}) copy-start(f32[128]{0:T(128)S(1)} %broadcast_multiply_fusion) | copy-start | bytes 1540
  156.8 11.2 %copy-start.34 = (f32[128]{0:T(128)}, f32[128]{0:T(128)S(1)}, u32[]{:S(2)}) copy-start(f32[128]{0:T(128)S(1)} %fusion.73) | copy-start | bytes 1540
  156.8 3.4 copy-start.16
  156.8 8.9 %slice-start = ((s8[4718592]{0:T(1024)(128)(4,1)}), s8[4194304]{0:T(1024)(128)(4,1)S(1)}, s32[]{:S(2)}) async-start(s8[4718592]{0:T(1024)(128)(4,1)} %bitcast.247), calls=%async_computation.9 | async-start | bytes 8388608
  160.2 5.5 copy-start.6
  160.2 5.5 slice-start.1
  165.7 2.3 copy-start.13
  168.0 1.8 copy-start.12
  168.0 2.5 copy-start.9
  178.7 11.6 %all-to-all-start.4 = ((bf16[16,2,3072]{2,1,0:T(2,128)(2,1)}), bf16[16,2,3072]{2,1,0:T(2,128)(2,1)}, u32[]{:S(2)}, u32[]{:S(2)}) async-start(bf16[16,2,3072]{2,1,0:T(2,128)(2,1)} %reshape.524), calls=%async_computation.4 | async-start | bytes 393216 | tf_op jit(solution)/shard_map/all_to_all | solution.py:234
  200.7 1.8 copy-start.14
  200.7 1.8 copy-start.24
  206.8 1.9 copy-start.5
  212.8 1.8 copy-start.24
  218.8 1.9 copy-start.5
  224.9 1.8 copy-start.14
  224.9 1.8 copy-start.24
  230.9 1.9 copy-start.5
  237.0 1.8 copy-start.14
  237.0 1.8 copy-start.24
  243.0 1.9 copy-start.5
  268.0 27.5 %all-to-all-start.5 = ((bf16[16,2,3072]{2,1,0:T(2,128)(2,1)}), bf16[16,2,3072]{2,1,0:T(2,128)(2,1)}, u32[]{:S(2)}, u32[]{:S(2)}) async-start(bf16[16,2,3072]{2,1,0:T(2,128)(2,1)} %reshape.530), calls=%async_computation.5 | async-start | bytes 393216 | tf_op jit(solution)/shard_map/all_to_all | solution.py:248
  295.6 32.7 %all-to-all-start.7 = ((bf16[16,2,3072]{2,1,0:T(2,128)(2,1)}), bf16[16,2,3072]{2,1,0:T(2,128)(2,1)}, u32[]{:S(2)}, u32[]{:S(2)}) async-start(bf16[16,2,3072]{2,1,0:T(2,128)(2,1)} %reshape.526), calls=%async_computation.7 | async-start | bytes 393216 | tf_op jit(solution)/shard_map/all_to_all | solution.py:250
  328.3 28.4 %all-to-all-start.6 = ((bf16[16,2,3072]{2,1,0:T(2,128)(2,1)}), bf16[16,2,3072]{2,1,0:T(2,128)(2,1)}, u32[]{:S(2)}, u32[]{:S(2)}) async-start(bf16[16,2,3072]{2,1,0:T(2,128)(2,1)} %reshape.528), calls=%async_computation.6 | async-start | bytes 393216 | tf_op jit(solution)/shard_map/all_to_all | solution.py:249
  335.1 280.8 %all-reduce.4.cloned.1.call-start = ((), (), s32[]{:S(2)}) async-start(), calls=%async_computation.8 | async-start | bytes 56623104 | tf_op jit(solution)/shard_map/psum | solution.py:260
  354.3 11.0 %copy-start.28 = (f32[128]{0:T(128)S(1)}, f32[128]{0:T(128)}, u32[]{:S(2)}) copy-start(f32[128]{0:T(128)} %copy-done.27) | copy-start | bytes 1540
  354.3 11.0 %copy-start.31 = (f32[128]{0:T(128)S(1)}, f32[128]{0:T(128)}, u32[]{:S(2)}) copy-start(f32[128]{0:T(128)} %copy-done.30) | copy-start | bytes 1540
  372.9 4.6 copy-start.18
  372.9 10.1 %copy-start.32 = (f32[128]{0:T(128)S(1)}, f32[128]{0:T(128)}, u32[]{:S(2)}) copy-start(f32[128]{0:T(128)} %copy-done.30) | copy-start | bytes 1540
  383.0 6.1 copy-start.29
  386.8 7.2 %copy-start.33 = (f32[768]{0:T(1024)S(1)}, f32[768]{0:T(1024)}, u32[]{:S(2)}) copy-start(f32[768]{0:T(1024)} %get-tuple-element.378) | copy-start | bytes 9220
  615.9 6.6 %copy-start.15 = (f32[768,768]{1,0:T(8,128)S(1)}, f32[768,768]{1,0:T(8,128)}, u32[]{:S(2)}) copy-start(f32[768,768]{1,0:T(8,128)} %get-tuple-element.611) | copy-start | bytes 7077892
  622.5 10.7 %slice-start.2 = ((s8[9437184]{0:T(1024)(128)(4,1)}), s8[4194304]{0:T(1024)(128)(4,1)S(1)}, s32[]{:S(2)}) async-start(s8[9437184]{0:T(1024)(128)(4,1)} %bitcast.249), calls=%async_computation.11 | async-start | bytes 8388608
  623.9 9.3 %slice-start.3 = ((s8[9437184]{0:T(1024)(128)(4,1)}), s8[4194304]{0:T(1024)(128)(4,1)S(1)}, s32[]{:S(2)}) async-start(s8[9437184]{0:T(1024)(128)(4,1)} %bitcast.249), calls=%async_computation.12 | async-start | bytes 8388608
  623.9 9.3 %slice-start.4 = ((s8[9437184]{0:T(1024)(128)(4,1)}), s8[1048576]{0:T(1024)(128)(4,1)S(1)}, s32[]{:S(2)}) async-start(s8[9437184]{0:T(1024)(128)(4,1)} %bitcast.249), calls=%async_computation.13 | async-start | bytes 2097152
  (29 other events, 31.8 us)
Sparse Core Ops, SparseCore 0:
  370.7 245.0 all-reduce.3
where the time goes:
time: 654 us; the launch traced here: 644 us
  local copies, waits for them, and re-layouts  157 us (24%)
  waiting for transfers between devices  154 us (24%)
  other arithmetic  97.6 us (15%)
  matrix products  89 us (14%)
  blocking collectives  72.1 us (11%)
  starting transfers between devices  53.8 us (8%)
  between operations  14.8 us (2%)
    psum x1, waiting for transfers between devices, local(): lax.psum((grad_ln1_gain, grad_ln1_bias, grad_w_qkv, grad_bias_query, grad...  150 us
    unnamed x102, local copies, waits for them, and re-layouts  77.7 us
    psum x1, blocking collectives, local(): lax.psum((grad_ln1_gain, grad_ln1_bias, grad_w_qkv, grad_bias_query, grad...  72.1 us
    unnamed x12, other arithmetic  67.5 us
    dot_general x4, matrix products, weight_grad(): jnp.einsum('rpd,rpe->de', left, right, preferred_element_type=jnp.float32)  21.4 us
    dot_general x8, matrix products, masked_scores(): jnp.einsum('qhd,khd->hqk', query_part, key_heads, preferred_element_type=...  16.7 us
  transfers between devices with their start and end apart: 9, of which 3 were waited for; matrix products, arithmetic and copies ran while one was open for 20% of the time, Pallas kernels for 0%

commit v1 on v0

v1 whole, which is shorter than its diff:
```python
import functools

import jax
import jax.numpy as jnp
from jax import lax
from jax.experimental import pallas as pl
from jax.experimental.pallas import tpu as pltpu
from jax.sharding import PartitionSpec as P

MESH = pl.DeviceIdType.MESH
f32 = jnp.float32
bf16 = jnp.bfloat16

D = 768
H = 16
FF = 3072
HS = 48
SEQ = 2048
TOK = 128
NB = 16
QB = 256
HALF_ROWS = 9216
PART_ROWS = 3072
SCALE = HS**-0.5
SCALE_LOG2E = SCALE * 1.4426950408889634
NEGATIVE = -1e30
EPSILON = 1e-05
GELU_C = 0.7978845608028654
GELU_A = 0.044715

LN1G, LN1B, BQ, BV, BOUT, LN2G, LN2B, BDOWN, BUP = 0, 1, 2, 3, 4, 5, 6, 7, 8
VROWS = 16


def dot(a, b):
    return jnp.dot(a, b, preferred_element_type=f32)


def dot_nt(a, b):
    return lax.dot_general(a, b, (((1,), (1,)), ((), ())), preferred_element_type=f32)


def turned(block):
    return jnp.transpose(block.astype(f32)).astype(bf16)


def coords():
    r = lax.axis_index("rows")
    s = lax.axis_index("seq")
    return lax.div(r, 2), lax.rem(r, 2), lax.div(s, 4), lax.rem(s, 4)


def device_at(y, c, z, x):
    return (y * 2 + c, z * 4 + x)


def remote(src, dst, send, recv, device):
    return pltpu.make_async_remote_copy(
        src_ref=src, dst_ref=dst, send_sem=send, recv_sem=recv, device_id=device, device_id_type=MESH
    )


def seq_peer(d):
    s = lax.axis_index("seq")
    return lax.rem(s + d, 16)


def axis_peer(axis, j):
    y, c, z, x = coords()
    if axis == "y":
        y = lax.rem(y + j, 4)
    elif axis == "z":
        z = lax.rem(z + j, 4)
    else:
        x = lax.rem(x + j, 4)
    return device_at(y, c, z, x)


def axis_place(axis):
    y, c, z, x = coords()
    return {"y": y, "z": z, "x": x}[axis]


def sibling():
    y, c, z, x = coords()
    return device_at(y, 1 - c, z, x)


def greet(with_seq, with_axes):
    bar = pltpu.get_barrier_semaphore()
    devices = [sibling()]
    if with_seq:
        r = lax.axis_index("rows")
        devices += [(r, seq_peer(d)) for d in range(1, 16)]
    for axis in with_axes:
        devices += [axis_peer(axis, j) for j in range(1, 4)]
    for device in devices:
        pl.semaphore_signal(bar, inc=1, device_id=device, device_id_type=MESH)
    return bar, len(devices)


def masked(scores, start, key0, query0, diagonal):
    key = lax.broadcasted_iota(jnp.int32, scores.shape, 0) + key0
    ok = key >= start
    if diagonal:
        query = lax.broadcasted_iota(jnp.int32, scores.shape, 1) + query0
        ok = ok & (key <= query)
    return jnp.where(ok, scores, NEGATIVE)


def segment_starts(offs_ref, query0, count):
    place = lax.broadcasted_iota(jnp.int32, (1, count), 1) + query0
    start = jnp.zeros((1, count), jnp.int32)
    for j in range(8):
        o = offs_ref[0, j]
        start = jnp.where(place >= o, o, start)
    return start


def pair(ref, i, lo, hi):
    return jnp.concatenate([ref[2 * i, lo:hi, :], ref[2 * i + 1, lo:hi, :]], axis=1)


def attend_forward(offs_ref, qkv, kn, vt, ot, lse, atts):
    for s in range(NB):
        kn[s * TOK : (s + 1) * TOK, :] = turned(qkv[s, 48:96, :])
        vt[:, s * TOK : (s + 1) * TOK] = qkv[s, 96:144, :]
    for i in range(SEQ // QB):
        q0 = i * QB
        qt = pair(qkv, i, 0, 48)
        start = segment_starts(offs_ref, q0, QB)
        sd = masked(dot(kn[q0 : q0 + QB, :], qt) * SCALE_LOG2E, start, q0, q0, True)
        top = jnp.max(sd, axis=0, keepdims=True)
        if i:
            so = masked(dot(kn[0:q0, :], qt) * SCALE_LOG2E, start, 0, q0, False)
            top = jnp.maximum(top, jnp.max(so, axis=0, keepdims=True))
        pd = jnp.exp2(sd - top)
        total = jnp.sum(pd, axis=0, keepdims=True)
        out = dot(vt[:, q0 : q0 + QB], pd.astype(bf16))
        if i:
            po = jnp.exp2(so - top)
            total = total + jnp.sum(po, axis=0, keepdims=True)
            out = out + dot(vt[:, 0:q0], po.astype(bf16))
        out = out / total
        ot[:, q0 : q0 + QB] = out
        lse[:, q0 : q0 + QB] = top + jnp.log2(total)
        low = out.astype(bf16)
        atts[2 * i] = low[:, 0:TOK]
        atts[2 * i + 1] = low[:, TOK:QB]


def attend_backward(offs_ref, qkv, kn, kt, vn, qn, don, dor, ot, lse, dqkv, dk, dv):
    for s in range(NB):
        rows = slice(s * TOK, (s + 1) * TOK)
        vn[rows, :] = turned(qkv[s, 96:144, :])
        qn[rows, :] = turned(qkv[s, 0:48, :])
        don[rows, :] = turned(dor[s])
        kt[:, rows] = qkv[s, 48:96, :]
    last = SEQ // QB - 1
    for i in reversed(range(SEQ // QB)):
        q0 = i * QB
        qt = pair(qkv, i, 0, 48)
        dot_t = pair(dor, i, 0, 48)
        start = segment_starts(offs_ref, q0, QB)
        level = lse[:, q0 : q0 + QB]
        inner = jnp.sum(dot_t.astype(f32) * ot[:, q0 : q0 + QB], axis=0, keepdims=True)
        q_n = qn[q0 : q0 + QB, :]
        do_n = don[q0 : q0 + QB, :]
        dq = None
        for a, b, diagonal in ([(0, q0, False)] if i else []) + [(q0, q0 + QB, True)]:
            scores = masked(dot(kn[a:b, :], qt) * SCALE_LOG2E, start, a, q0, diagonal)
            probs = jnp.exp2(scores - level)
            dp = dot(vn[a:b, :], dot_t)
            ds = (probs * (dp - inner)).astype(bf16)
            dv_part = dot(probs.astype(bf16), do_n)
            dk_part = dot(ds, q_n)
            if i == last:
                dk[a:b, :] = dk_part
                dv[a:b, :] = dv_part
            else:
                dk[a:b, :] += dk_part
                dv[a:b, :] += dv_part
            dq_part = dot(kt[:, a:b], ds)
            dq = dq_part if dq is None else dq + dq_part
        dq = (dq * SCALE).astype(bf16)
        for h in range(2):
            s = 2 * i + h
            rows = slice(s * TOK, (s + 1) * TOK)
            dqkv[s, 0:48, :] = dq[:, h * TOK : (h + 1) * TOK]
            dqkv[s, 48:96, :] = (jnp.transpose(dk[rows, :]) * SCALE).astype(bf16)
            dqkv[s, 96:144, :] = jnp.transpose(dv[rows, :]).astype(bf16)


def norm_parts(values):
    center = values - jnp.mean(values, axis=-1, keepdims=True)
    spread = jnp.mean(center * center, axis=-1, keepdims=True)
    rs = lax.rsqrt(spread + EPSILON)
    return center * rs, rs


def norm_back(grad, n, rs, gain):
    gg = grad * gain
    return rs * (
        gg - jnp.mean(gg, axis=-1, keepdims=True) - n * jnp.mean(gg * n, axis=-1, keepdims=True)
    )


def over_tokens(values):
    return jnp.sum(values, axis=0, keepdims=True)


def exchange(src, dst, send, recv):
    r = lax.axis_index("rows")
    s = lax.axis_index("seq")
    copies = []
    for d in range(1, 16):
        peer = seq_peer(d)
        copy = remote(src.at[peer], dst.at[s], send.at[d], recv.at[d], (r, peer))
        copy.start()
        copies.append(copy)
    dst[s] = src[s]
    return copies


def block_kernel(
    offs, x_ref, dy_ref, vec, wqkv_h, wout_h, wup_h, wdown_h,
    out_ref, ig_ref, g_ref, vecg,
    wqkv, wout, wup, wdown, wsem,
    qkvt, rqkv, kn, vt, ot, lse, atts, ratt,
    h1t, h1ts, n1, rs1, h2t, h2ts, dys, actt, actts, gp, gps, gb, gbs, attts, gres,
    gattt, rda, kt, vn, qn, don, dk, dv, dqkv, rdq, dqs,
    asend, arecv, ssend, srecv,
):
    bar, count = greet(True, ())
    loads = []
    for n, (src, dst) in enumerate(((wqkv_h, wqkv), (wout_h, wout), (wup_h, wup), (wdown_h, wdown))):
        load = pltpu.make_async_copy(src, dst, wsem.at[n])
        load.start()
        loads.append(load)

    core = lax.rem(lax.axis_index("rows"), 2)
    other = 1 - core
    sib = sibling()
    to_sib = []

    def send_sib(n, src, dst):
        copy = remote(src, dst, ssend.at[n], srecv.at[n], sib)
        copy.start()
        to_sib.append(copy)

    x = x_ref[...].astype(f32)
    n, rs = norm_parts(x)
    n1[...] = n
    rs1[...] = rs
    h1f = n * vec[LN1G : LN1G + 1, :] + vec[LN1B : LN1B + 1, :]
    h1 = h1f.astype(bf16)
    h1t[...] = jnp.transpose(h1f).astype(bf16)
    loads[0].wait()
    for t in range(3):
        y = dot(h1, wqkv[:, t * D : (t + 1) * D])
        if t == 0:
            y = y + vec[BQ : BQ + 1, :]
        if t == 2:
            y = y + vec[BV : BV + 1, :]
        qkvt[:, t * HS : (t + 1) * HS, :] = jnp.transpose(y).astype(bf16).reshape(H, HS, TOK)
    pl.semaphore_wait(bar, count)
    moved = exchange(qkvt, rqkv, asend.at[0], arecv.at[0])
    send_sib(0, h1t, h1ts)
    send_sib(1, dy_ref, dys)
    for copy in moved:
        copy.wait()

    attend_forward(offs, rqkv, kn, vt, ot, lse, atts)
    moved = exchange(atts, ratt, asend.at[1], arecv.at[1])
    for load in loads[1:]:
        load.wait()
    for copy in moved:
        copy.wait()

    att = jnp.transpose(ratt[...].reshape(D, TOK).astype(f32)).astype(bf16)
    send_sib(2, ratt.at[pl.ds(other * 8, 8)], attts)
    resid = x_ref[...].astype(f32) + dot(att, wout[...]) + vec[BOUT : BOUT + 1, :]
    n2, rs2 = norm_parts(resid)
    h2f = n2 * vec[LN2G : LN2G + 1, :] + vec[LN2B : LN2B + 1, :]
    h2 = h2f.astype(bf16)
    h2t[...] = jnp.transpose(h2f).astype(bf16)
    send_sib(3, h2t, h2ts)
    dy = dy_ref[...]
    down = None
    dh2 = None
    for c in range(4):
        cols = slice(c * D, (c + 1) * D)
        pre = dot(h2, wup[:, cols]) + vec[BUP + c : BUP + c + 1, :]
        square = pre * pre
        t = jnp.tanh(GELU_C * (pre + GELU_A * (square * pre)))
        act = 0.5 * pre * (1.0 + t)
        slope = 0.5 * (1.0 + t) + (0.5 * GELU_C) * pre * (1.0 - t * t) * (1.0 + (3.0 * GELU_A) * square)
        part = dot(act.astype(bf16), wdown[cols, :])
        down = part if down is None else down + part
        actt[c] = jnp.transpose(act).astype(bf16)
        gpre = (dot_nt(dy, wdown[cols, :]) * slope).astype(bf16)
        gp[c] = gpre
        vecg[BUP + c : BUP + c + 1, :] = over_tokens(gpre.astype(f32))
        part = dot_nt(gpre, wup[:, cols])
        dh2 = part if dh2 is None else dh2 + part
    send_sib(4, actt.at[pl.ds(other * 2, 2)], actts)
    send_sib(5, gp.at[pl.ds(other * 2, 2)], gps)
    out_ref[...] = (resid + down + vec[BDOWN : BDOWN + 1, :]).astype(bf16)
    vecg[BDOWN : BDOWN + 1, :] = over_tokens(dy.astype(f32))
    vecg[LN2G : LN2G + 1, :] = over_tokens(dh2 * n2)
    vecg[LN2B : LN2B + 1, :] = over_tokens(dh2)
    grad = dy.astype(f32) + norm_back(dh2, n2, rs2, vec[LN2G : LN2G + 1, :])
    gres[...] = grad
    branch = grad.astype(bf16)
    gb[...] = branch
    vecg[BOUT : BOUT + 1, :] = over_tokens(branch.astype(f32))
    gattt[...] = jnp.transpose(dot_nt(branch, wout[...])).astype(bf16).reshape(H, HS, TOK)
    moved = exchange(gattt, rda, asend.at[2], arecv.at[2])
    send_sib(6, gb, gbs)

    for k in (1, 2, 3, 4, 5, 6):
        to_sib[k].wait()
    dy2 = jnp.concatenate([dy, dys[...]], axis=0)
    for j in range(2):
        left = jnp.concatenate([actt[core * 2 + j], actts[j]], axis=1)
        res = dot(left, dy2).astype(bf16)
        for t in range(6):
            lo = t * 1536 + j * D
            g_ref[0, lo : lo + D, :] = res[:, t * TOK : (t + 1) * TOK]
    left = jnp.concatenate([h2t[...], h2ts[...]], axis=1)
    for j in range(2):
        right = jnp.concatenate([gp[core * 2 + j], gps[j]], axis=0)
        res = dot(left, right).astype(bf16)
        for t in range(6):
            lo = (j * 6 + t) * D
            g_ref[1, lo : lo + D, :] = res[:, t * TOK : (t + 1) * TOK]
    left = jnp.concatenate(
        [ratt[pl.ds(core * 8, 8)].reshape(384, TOK), attts[...].reshape(384, TOK)], axis=1
    )
    right = jnp.concatenate([gb[...], gbs[...]], axis=0)
    res = dot(left, right).astype(bf16)
    for t in range(6):
        lo = 6912 + t * 384
        g_ref[2, lo : lo + 384, :] = res[:, t * TOK : (t + 1) * TOK]

    for copy in moved:
        copy.wait()
    attend_backward(offs, rqkv, kn, kt, vn, qn, don, rda, ot, lse, dqkv, dk, dv)
    moved = exchange(dqkv, rdq, asend.at[3], arecv.at[3])
    for copy in moved:
        copy.wait()
    send_sib(7, rdq.at[pl.ds(other * 8, 8)], dqs)

    dh1t = None
    ones = jnp.ones((8, TOK), bf16)
    for t in range(3):
        grad_t = rdq[:, t * HS : (t + 1) * HS, :].reshape(D, TOK)
        part = dot(wqkv[:, t * D : (t + 1) * D], grad_t)
        dh1t = part if dh1t is None else dh1t + part
        if t != 1:
            row = BQ if t == 0 else BV
            vecg[row : row + 1, :] = dot_nt(ones, grad_t)[0:1, :]
    dh1 = jnp.transpose(dh1t)
    n = n1[...]
    vecg[LN1G : LN1G + 1, :] = over_tokens(dh1 * n)
    vecg[LN1B : LN1B + 1, :] = over_tokens(dh1)
    vecg[12:16, :] = jnp.zeros((4, D), f32)
    ig_ref[...] = (gres[...] + norm_back(dh1, n, rs1[...], vec[LN1G : LN1G + 1, :])).astype(bf16)

    to_sib[0].wait()
    to_sib[7].wait()
    left = jnp.concatenate([h1t[...], h1ts[...]], axis=1)
    for t in range(3):
        mine = rdq[pl.ds(core * 8, 8), t * HS : (t + 1) * HS, :].reshape(384, TOK)
        theirs = dqs[:, t * HS : (t + 1) * HS, :].reshape(384, TOK)
        res = dot_nt(left, jnp.concatenate([mine, theirs], axis=1)).astype(bf16)
        for u in range(3):
            lo = (t * 3 + u) * D
            g_ref[2, lo : lo + D, :] = res[:, u * TOK : (u + 1) * TOK]


VMEM = pl.BlockSpec(memory_space=pltpu.VMEM)
SMEM = pl.BlockSpec(memory_space=pltpu.SMEM)
ANY = pl.BlockSpec(memory_space=pl.ANY)


def call_block(offsets, x, dy, vec, w_qkv, w_out, w_up, w_down):
    v = pltpu.VMEM
    dma = pltpu.SemaphoreType.DMA
    shape = jax.ShapeDtypeStruct
    return pl.pallas_call(
        block_kernel,
        out_shape=(
            shape((TOK, D), bf16),
            shape((TOK, D), bf16),
            shape((3, HALF_ROWS, TOK), bf16),
            shape((VROWS, D), f32),
        ),
        in_specs=[SMEM, VMEM, VMEM, VMEM, ANY, ANY, ANY, ANY],
        out_specs=(VMEM, VMEM, VMEM, VMEM),
        scratch_shapes=[
            v((D, 3 * D), bf16), v((D, D), bf16), v((D, FF), bf16), v((FF, D), bf16), dma((4,)),
            v((NB, 144, TOK), bf16), v((NB, 144, TOK), bf16), v((SEQ, HS), bf16), v((HS, SEQ), bf16),
            v((HS, SEQ), f32), v((1, SEQ), f32), v((NB, HS, TOK), bf16), v((NB, HS, TOK), bf16),
            v((D, TOK), bf16), v((D, TOK), bf16), v((TOK, D), f32), v((TOK, 1), f32),
            v((D, TOK), bf16), v((D, TOK), bf16), v((TOK, D), bf16),
            v((4, D, TOK), bf16), v((2, D, TOK), bf16), v((4, TOK, D), bf16), v((2, TOK, D), bf16),
            v((TOK, D), bf16), v((TOK, D), bf16), v((8, HS, TOK), bf16), v((TOK, D), f32),
            v((NB, HS, TOK), bf16), v((NB, HS, TOK), bf16),
            v((HS, SEQ), bf16), v((SEQ, HS), bf16), v((SEQ, HS), bf16), v((SEQ, HS), bf16),
            v((SEQ, HS), f32), v((SEQ, HS), f32),
            v((NB, 144, TOK), bf16), v((NB, 144, TOK), bf16), v((8, 144, TOK), bf16),
            dma((4, 16)), dma((4, 16)), dma((8,)), dma((8,)),
        ],
        compiler_params=pltpu.CompilerParams(
            collective_id=1, has_side_effects=True, vmem_limit_bytes=58 * 2**20
        ),
    )(offsets, x, dy, vec, w_qkv, w_out, w_up, w_down)


ORDERS = (("x", "y", "z"), ("y", "z", "x"), ("z", "x", "y"))


def sum_kernel(
    g_ref, vecg, ag, vecs,
    recv1, buf2, recv2, buf3, recv3, buf4, vbuf, vrecv,
    s1, r1, s2, r2, s3, r3, t3, u3, t2, u2, t1, u1, own, fs, fr, vs, vr,
):
    bar, count = greet(False, ("x", "y", "z"))
    core = lax.rem(lax.axis_index("rows"), 2)
    sib = sibling()
    place = [[axis_place(a) for a in order] for order in ORDERS]
    pl.semaphore_wait(bar, count)

    def fan(send, recv, g, p, axis, pick):
        copies = []
        for j in range(1, 4):
            there = lax.rem(place[p][axis] + j, 4)
            src, dst = pick(j, there)
            copy = remote(src, dst, send.at[g, p, j - 1], recv.at[g, p, j - 1], axis_peer(ORDERS[p][axis], j))
            copy.start()
            copies.append(copy)
        return copies

    def wait(copies):
        for copy in copies:
            copy.wait()

    def total(first, rest):
        acc = first.astype(f32)
        for j in range(3):
            acc = acc + rest[j].astype(f32)
        return acc.astype(bf16)

    def start1(g, p):
        base = p * PART_ROWS
        return fan(s1, r1, g, p, 0, lambda j, q: (g_ref.at[g, pl.ds(base + q * 768, 768)], recv1.at[g, p, j - 1]))

    def start2(g, p):
        lo = p * PART_ROWS + place[p][0] * 768
        buf2[g, p] = total(g_ref[g, pl.ds(lo, 768)], recv1[g, p])
        return fan(s2, r2, g, p, 1, lambda j, q: (buf2.at[g, p, pl.ds(q * 192, 192)], recv2.at[g, p, j - 1]))

    def start3(g, p):
        buf3[g, p] = total(buf2[g, p, pl.ds(place[p][1] * 192, 192)], recv2[g, p])
        return fan(s3, r3, g, p, 2, lambda j, q: (buf3.at[g, p, pl.ds(q * 48, 48)], recv3.at[g, p, j - 1]))

    def back3(g, p):
        buf4[g, p] = total(buf3[g, p, pl.ds(place[p][2] * 48, 48)], recv3[g, p])
        lo = p * PART_ROWS + (place[p][0] * 16 + place[p][1] * 4 + place[p][2]) * 48
        spot = ag.at[core, g, pl.ds(lo, 48)]
        copies = fan(t3, u3, g, p, 2, lambda j, q: (buf4.at[g, p], spot))
        mine = pltpu.make_async_copy(buf4.at[g, p], spot, own.at[g, p])
        mine.start()
        return copies + [mine]

    def back2(g, p):
        lo = p * PART_ROWS + (place[p][0] * 16 + place[p][1] * 4) * 48
        spot = ag.at[core, g, pl.ds(lo, 192)]
        return fan(t2, u2, g, p, 1, lambda j, q: (spot, spot))

    def back1(g, p):
        spot = ag.at[core, g, pl.ds(p * PART_ROWS + place[p][0] * 768, 768)]
        return fan(t1, u1, g, p, 0, lambda j, q: (spot, spot))

    def forward(g, p):
        spot = ag.at[core, g, pl.ds(p * PART_ROWS, PART_ROWS)]
        copy = remote(spot, spot, fs.at[g, p], fr.at[g, p], sib)
        copy.start()
        return [copy]

    def vec_start(k, axis):
        copies = []
        for j in range(1, 4):
            copy = remote(vbuf.at[k], vrecv.at[k, j - 1], vs.at[k, j - 1], vr.at[k, j - 1], axis_peer(axis, j))
            copy.start()
            copies.append(copy)
        return copies

    def vec_sum(k):
        return vbuf[k] + vrecv[k, 0] + vrecv[k, 1] + vrecv[k, 2]

    vbuf[0] = vecg[...]
    small = vec_start(0, "x")

    stages = [start1, start2, start3, back3, back2, back1, forward]
    live = {}
    steps = len(stages)
    for tick in range(steps + 2):
        for g in range(3):
            k = tick - g
            if g == 0 and tick == 0:
                for gg in range(3):
                    for p in range(3):
                        live[gg, p] = start1(gg, p)
            if k < 1 or k >= steps:
                continue
            for p in range(3):
                wait(live[g, p])
                live[g, p] = stages[k](g, p)
        if tick in (1, 2):
            wait(small)
            vbuf[tick] = vec_sum(tick - 1)
            small = vec_start(tick, ("x", "y", "z")[tick])
        if tick == 3:
            wait(small)
            vbuf[3] = vec_sum(2)
            pair_copy = remote(vbuf.at[3], vrecv.at[3, 0], vs.at[3, 0], vr.at[3, 0], sib)
            pair_copy.start()
            small = [pair_copy]
        if tick == 4:
            wait(small)
            vecs[...] = vbuf[3] + vrecv[3, 0]
    for g in range(3):
        for p in range(3):
            wait(live[g, p])


def call_sum(g, vecg):
    v = pltpu.VMEM
    dma = pltpu.SemaphoreType.DMA
    shape = jax.ShapeDtypeStruct
    d3 = dma((3, 3, 3))
    return pl.pallas_call(
        sum_kernel,
        out_shape=(shape((2, 3, HALF_ROWS, TOK), bf16), shape((VROWS, D), f32)),
        in_specs=[VMEM, VMEM],
        out_specs=(ANY, VMEM),
        scratch_shapes=[
            v((3, 3, 3, 768, TOK), bf16), v((3, 3, 768, TOK), bf16), v((3, 3, 3, 192, TOK), bf16),
            v((3, 3, 192, TOK), bf16), v((3, 3, 3, 48, TOK), bf16), v((3, 3, 48, TOK), bf16),
            v((4, VROWS, D), f32), v((4, 3, VROWS, D), f32),
            d3, d3, d3, d3, d3, d3, d3, d3, d3, d3, d3, d3, dma((3, 3)), dma((3, 3)), dma((3, 3)),
            dma((4, 3)), dma((4, 3)),
        ],
        compiler_params=pltpu.CompilerParams(
            collective_id=2, has_side_effects=True, vmem_limit_bytes=58 * 2**20
        ),
    )(g, vecg)


def widen_kernel(ag, vecs, wqkv, wout, wup, wdown, *rest):
    small, (inb, outb, isem, osem) = rest[:9], rest[9:]
    for ref, row in zip(small, (LN1G, LN1B, BQ, BV, BOUT, LN2G, LN2B, None, BDOWN)):
        if row is None:
            for c in range(4):
                ref[:, c * D : (c + 1) * D] = vecs[BUP + c : BUP + c + 1, :]
        else:
            ref[...] = vecs[row : row + 1, :]
    tasks = []
    for c in range(2):
        for j in range(2):
            for h in range(2):
                rows = [(0, (h * 3 + t) * 1536 + j * D) for t in range(3)]
                tasks.append((c, rows, wdown.at[pl.ds(c * 1536 + j * D, D), pl.ds(h * 384, 384)]))
        for h in range(4):
            rows = [(1, (h * 3 + t) * D) for t in range(3)]
            tasks.append((c, rows, wup.at[:, pl.ds(c * 1536 + h * 384, 384)]))
        for h in range(3):
            rows = [(2, (h * 3 + t) * D) for t in range(3)]
            tasks.append((c, rows, wqkv.at[:, pl.ds(h * D + c * 384, 384)]))
        for h in range(2):
            rows = [(2, 6912 + (h * 3 + t) * 384) for t in range(3)]
            tasks.append((c, rows, wout.at[pl.ds(c * 384, 384), pl.ds(h * 384, 384)]))
    slots = 4

    def height(k):
        return 384 if tasks[k][2].shape[0] == 384 else D

    def load(k):
        c, rows, _ = tasks[k]
        size = height(k)
        for t, (g, lo) in enumerate(rows):
            pltpu.make_async_copy(
                ag.at[c, g, pl.ds(lo, size)], inb.at[k % slots, t, pl.ds(0, size)], isem.at[k % slots, t]
            ).start()

    def load_wait(k):
        c, rows, _ = tasks[k]
        size = height(k)
        for t, (g, lo) in enumerate(rows):
            pltpu.make_async_copy(
                ag.at[c, g, pl.ds(lo, size)], inb.at[k % slots, t, pl.ds(0, size)], isem.at[k % slots, t]
            ).wait()

    def store(k):
        return pltpu.make_async_copy(
            outb.at[k % slots, pl.ds(0, height(k))], tasks[k][2], osem.at[k % slots]
        )

    for k in range(slots - 1):
        load(k)
    for k in range(len(tasks)):
        if k + slots - 1 < len(tasks):
            load(k + slots - 1)
        load_wait(k)
        if k >= slots:
            store(k - slots).wait()
        size = height(k)
        for t in range(3):
            outb[k % slots, 0:size, t * TOK : (t + 1) * TOK] = inb[k % slots, t, 0:size, :].astype(f32)
        store(k).start()
    for k in range(len(tasks) - slots, len(tasks)):
        store(k).wait()


def call_widen(ag, vecs):
    v = pltpu.VMEM
    dma = pltpu.SemaphoreType.DMA
    shape = jax.ShapeDtypeStruct
    return pl.pallas_call(
        widen_kernel,
        out_shape=(
            shape((D, 3 * D), f32), shape((D, D), f32), shape((D, FF), f32), shape((FF, D), f32),
        ) + tuple(shape((1, FF if k == 7 else D), f32) for k in range(9)),
        in_specs=[ANY, VMEM],
        out_specs=(ANY,) * 4 + (VMEM,) * 9,
        scratch_shapes=[v((4, 3, D, TOK), bf16), v((4, D, 384), f32), dma((4, 3)), dma((4,))],
        compiler_params=pltpu.CompilerParams(vmem_limit_bytes=40 * 2**20),
    )(ag, vecs)


def local(
    block_input, offsets, ln1_gain, ln1_bias, w_qkv, bias_query, bias_value, w_out, bias_out,
    ln2_gain, ln2_bias, w_up, bias_up, w_down, bias_down, cotangent,
):
    vec = jnp.concatenate(
        [ln1_gain, ln1_bias, bias_query, bias_value, bias_out, ln2_gain, ln2_bias, bias_down, bias_up]
    ).astype(f32).reshape(12, D)
    out, ig, g, vecg = call_block(
        offsets, block_input.reshape(TOK, D), cotangent.reshape(TOK, D), vec, w_qkv, w_out, w_up, w_down
    )
    ag, vecs = call_sum(g, vecg)
    wide = call_widen(ag, vecs)
    g_qkv, g_out, g_up, g_down = wide[:4]
    s = [item.reshape(-1) for item in wide[4:]]
    return (
        out.reshape(1, TOK, D), ig.reshape(1, TOK, D),
        s[0], s[1], g_qkv, s[2], s[3], g_out, s[4], s[5], s[6], g_up, s[7], g_down, s[8],
    )


def solution(mesh):
    tokens = P("rows", "seq", None)
    return jax.shard_map(
        local,
        mesh=mesh,
        in_specs=(tokens, P("rows", None)) + (P(),) * 13 + (tokens,),
        out_specs=(tokens, tokens) + (P(),) * 13,
        check_vma=False,
    )
```

time: 654 us -> 197 us (0.30); the launches traced: 644 us -> 196 us
  Pallas kernels: 0 us -> 176 us
  waiting for transfers between devices: 154 us -> 0 us
  local copies, waits for them, and re-layouts: 157 us -> 15.4 us
  other arithmetic: 97.6 us -> 4.84 us
  matrix products: 89 us -> 0 us
  blocking collectives: 72.1 us -> 0 us
  starting transfers between devices: 53.8 us -> 0 us
  between operations: 14.8 us -> 0.7 us
    pallas_call x0 -> x3, Pallas kernels: none -> 176 us  [the longest x1 92.3 us: call_sum(): pl.pallas_call(sum_kernel, out_shape=(shape((2, 3, HALF_ROWS, TOK), bf16)...]
    psum x1 -> x0, waiting for transfers between devices: 150 us -> none  [local(): lax.psum((grad_ln1_gain, grad_ln1_bias, grad_w_qkv, grad_bias_query, grad...]
    dot_general x40 -> x0, matrix products: 89 us -> none  [the longest x4 21.4 us: weight_grad(): jnp.einsum('rpd,rpe->de', left, right, preferred_element_type=jnp.float32)]
    psum x1 -> x0, blocking collectives: 72.1 us -> none  [local(): lax.psum((grad_ln1_gain, grad_ln1_bias, grad_w_qkv, grad_bias_query, grad...]
    unnamed x12 -> x1, other arithmetic: 67.5 us -> 0.01 us
    unnamed x102 -> x18, local copies, waits for them, and re-layouts: 77.7 us -> 14 us
    all_to_all x8 -> x0, starting transfers between devices: 53.8 us -> none  [the longest x1 8.61 us: local(): lax.all_to_all(value_rows, 'seq', split_axis=2, concat_axis=1, tiled=True)]
    reduce_sum x16 -> x0, other arithmetic: 17.5 us -> none  [the longest x4 6.05 us: token_sum(): return jnp.sum(values.astype(jnp.float32), axis=(0, 1))]
  transfers between devices with their start and end apart: 9 -> 0, of which waited for: 3 -> 0; matrix products, arithmetic and copies ran while one was open for 20% -> 0% of each run, Pallas kernels for 0% -> 0%
where the time goes in v1:
time: 197 us; the launch traced here: 196 us
  Pallas kernels  176 us (89%)
  local copies, waits for them, and re-layouts  15.4 us (8%)
  other arithmetic  4.84 us (2%)
    pallas_call x1, Pallas kernels, call_sum(): pl.pallas_call(sum_kernel, out_shape=(shape((2, 3, HALF_ROWS, TOK), bf16)...  92.3 us
    pallas_call x1, Pallas kernels, call_block(): pl.pallas_call(block_kernel, out_shape=(shape((TOK, D), bf16), shape((TOK...  60.9 us
    pallas_call x1, Pallas kernels, call_widen(): pl.pallas_call(widen_kernel, out_shape=(shape((D, 3 * D), f32), shape((D,...  22.5 us
    unnamed x18, local copies, waits for them, and re-layouts  14 us
    pallas_call x8, other arithmetic, call_widen(): pl.pallas_call(widen_kernel, out_shape=(shape((D, 3 * D), f32), shape((D,...  4.84 us

profile of v1, /device:TPU:1, one launch (start us, length us, event | category | flops | bytes accessed | tf_op | source)
XLA Modules:
  0.0 196.5 jit_solution(5469599251305372185)
XLA Ops:
  0.7 0.9 dynamic-update-slice
  1.5 0.8 dynamic-update-slice.1
  2.4 0.9 dynamic-update-slice.2
  3.2 0.9 dynamic-update-slice.3
  4.1 0.9 dynamic-update-slice.4
  4.9 0.8 dynamic-update-slice.5
  5.8 0.9 dynamic-update-slice.6
  6.6 0.9 dynamic-update-slice.7
  7.5 0.7 constant_dynamic-update-slice_fusion
  8.2 0.7 reshape.86.vec
  8.8 60.9 %shard_map.271 = (bf16[128,768]{1,0:T(8,128)(2,1)}, bf16[128,768]{1,0:T(8,128)(2,1)}, bf16[3,9216,128]{2,1,0:T(8,128)(2,1)}, f32[16,768]{1,0:T(8,128)}) custom-call(s32[1,8]{1,0:T(1,128)} %offs.1, bf16[128,768]{1,0:T(8,128)(2,1)} %bitcast.5, bf16[128,768]{1,0:T(8,128)(2,1)} %bitcast.6, f32[12,768]{1,0:T(8,128)} %reshape.86.vec, bf16[768,2304]{1,0:T(8,128)(2,1)} %wqkv_h.1, ...), custom_call_target="tpu_custom_call" | custom-call | tf_op jit(solution)/shard_map/pallas_call | solution.py:391
  69.7 92.3 %shard_map.272 = (bf16[2,3,9216,128]{3,2,1,0:T(8,128)(2,1)}, f32[16,768]{1,0:T(8,128)}) custom-call(bf16[3,9216,128]{2,1,0:T(8,128)(2,1)} %get-tuple-element.36.g_ref, f32[16,768]{1,0:T(8,128)} %get-tuple-element.37.vecg), custom_call_target="tpu_custom_call" | custom-call | tf_op jit(solution)/shard_map/pallas_call | solution.py:544
  162.0 0.0 copy-start
  162.0 5.0 %copy-done = bf16[2,3,9216,128]{3,2,1,0:T(8,128)(2,1)S(1)} copy-done((bf16[2,3,9216,128]{3,2,1,0:T(8,128)(2,1)S(1)}, bf16[2,3,9216,128]{3,2,1,0:T(8,128)(2,1)}, u32[]{:S(2)}) %copy-start) | copy-done | bytes 14155800
  167.0 0.0 copy-start.1
  167.0 0.8 copy-done.1
  167.8 0.0 copy-start.3
  167.8 0.0 copy-start.2
  167.8 22.5 %shard_map.273 = (f32[768,2304]{1,0:T(8,128)}, f32[768,768]{1,0:T(8,128)}, f32[768,3072]{1,0:T(8,128)}, f32[3072,768]{1,0:T(8,128)}, f32[1,768]{1,0:T(1,128)S(1)...) custom-call(bf16[2,3,9216,128]{3,2,1,0:T(8,128)(2,1)S(1)} %copy-done, ...), custom_call_target="tpu_custom_call" | custom-call | tf_op jit(solution)/shard_map/pallas_call | solution.py:631
  190.3 0.6 reduce
  190.9 0.6 reduce.1
  191.5 0.6 reduce.2
  192.1 0.6 reduce.3
  192.7 0.6 reduce.4
  193.3 0.6 reduce.5
  193.9 0.6 reduce.6
  194.5 0.6 reduce.7
  195.1 0.0 copy-done.3
  195.1 0.7 copy.42
  195.8 0.0 copy-done.2
  195.8 0.7 copy.43
  (1 shorter events, 0.0 us)
Async XLA Ops:
  162.0 5.0 %copy-start = (bf16[2,3,9216,128]{3,2,1,0:T(8,128)(2,1)S(1)}, bf16[2,3,9216,128]{3,2,1,0:T(8,128)(2,1)}, u32[]{:S(2)}) copy-start(bf16[2,3,9216,128]{3,2,1,0:T(8,128)(2,1)} %get-tuple-element.38.ag) | copy-start | bytes 42467332
  167.0 0.8 copy-start.1
  167.8 27.3 %copy-start.3 = (bf16[128,768]{1,0:T(8,128)(2,1)S(1)}, bf16[128,768]{1,0:T(8,128)(2,1)}, u32[]{:S(2)}) copy-start(bf16[128,768]{1,0:T(8,128)(2,1)} %get-tuple-element.34) | copy-start | bytes 589828
  167.8 28.0 %copy-start.2 = (bf16[128,768]{1,0:T(8,128)(2,1)S(1)}, bf16[128,768]{1,0:T(8,128)(2,1)}, u32[]{:S(2)}) copy-start(bf16[128,768]{1,0:T(8,128)(2,1)} %get-tuple-element.35) | copy-start | bytes 589828

commit v2 on v1

v2 whole, which is shorter than its diff:
```python
import functools

import jax
import jax.numpy as jnp
from jax import lax
from jax.experimental import pallas as pl
from jax.experimental.pallas import tpu as pltpu
from jax.sharding import PartitionSpec as P

MESH = pl.DeviceIdType.MESH
f32 = jnp.float32
bf16 = jnp.bfloat16

D = 768
H = 16
FF = 3072
HS = 48
SEQ = 2048
TOK = 128
NB = 16
QB = 256
GROUP_ROWS = (9216, 11520, 6912)
OUT_ROW = 9216
ALL_ROWS = sum(GROUP_ROWS)
SCALE = HS**-0.5
SCALE_LOG2E = SCALE * 1.4426950408889634
NEGATIVE = -1e30
EPSILON = 1e-05
GELU_C = 0.7978845608028654
GELU_A = 0.044715

LN1G, LN1B, BQ, BV = 0, 1, 2, 3
BOUT, LN2G, LN2B, BDOWN, BUP = 0, 1, 2, 3, 4
VROWS = 8
WIDEN_SLOTS = 6


def dot(a, b):
    return jnp.dot(a, b, preferred_element_type=f32)


def dot_nt(a, b):
    return lax.dot_general(a, b, (((1,), (1,)), ((), ())), preferred_element_type=f32)


def turned(block):
    return jnp.transpose(block.astype(f32)).astype(bf16)


def coords():
    r = lax.axis_index("rows")
    s = lax.axis_index("seq")
    return lax.div(r, 2), lax.rem(r, 2), lax.div(s, 4), lax.rem(s, 4)


def device_at(y, c, z, x):
    return (y * 2 + c, z * 4 + x)


def remote(src, dst, send, recv, device):
    return pltpu.make_async_remote_copy(
        src_ref=src, dst_ref=dst, send_sem=send, recv_sem=recv, device_id=device, device_id_type=MESH
    )


def seq_peer(d):
    s = lax.axis_index("seq")
    return lax.rem(s + d, 16)


def axis_peer(axis, j):
    y, c, z, x = coords()
    if axis == "y":
        y = lax.rem(y + j, 4)
    elif axis == "z":
        z = lax.rem(z + j, 4)
    else:
        x = lax.rem(x + j, 4)
    return device_at(y, c, z, x)


def axis_place(axis):
    y, c, z, x = coords()
    return {"y": y, "z": z, "x": x}[axis]


def sibling():
    y, c, z, x = coords()
    return device_at(y, 1 - c, z, x)


def greet(with_seq, with_axes):
    bar = pltpu.get_barrier_semaphore()
    devices = [sibling()]
    if with_seq:
        r = lax.axis_index("rows")
        devices += [(r, seq_peer(d)) for d in range(1, 16)]
    for axis in with_axes:
        devices += [axis_peer(axis, j) for j in range(1, 4)]
    for device in devices:
        pl.semaphore_signal(bar, inc=1, device_id=device, device_id_type=MESH)
    return bar, len(devices)


def masked(scores, start, key0, query0, diagonal):
    key = lax.broadcasted_iota(jnp.int32, scores.shape, 0) + key0
    ok = key >= start
    if diagonal:
        query = lax.broadcasted_iota(jnp.int32, scores.shape, 1) + query0
        ok = ok & (key <= query)
    return jnp.where(ok, scores, NEGATIVE)


def segment_starts(offs_ref, query0, count):
    place = lax.broadcasted_iota(jnp.int32, (1, count), 1) + query0
    start = jnp.zeros((1, count), jnp.int32)
    for j in range(8):
        o = offs_ref[0, j]
        start = jnp.where(place >= o, o, start)
    return start


def pair(ref, i, lo, hi):
    return jnp.concatenate([ref[2 * i, lo:hi, :], ref[2 * i + 1, lo:hi, :]], axis=1)


def attend_forward(offs_ref, qk, vals, kn, vt, ot, lse, atts, after):
    for s in range(NB):
        kn[s * TOK : (s + 1) * TOK, :] = turned(qk[s, 48:96, :])
        vt[:, s * TOK : (s + 1) * TOK] = vals[s]
    for i in range(SEQ // QB):
        q0 = i * QB
        qt = pair(qk, i, 0, 48)
        start = segment_starts(offs_ref, q0, QB)
        sd = masked(dot(kn[q0 : q0 + QB, :], qt) * SCALE_LOG2E, start, q0, q0, True)
        top = jnp.max(sd, axis=0, keepdims=True)
        if i:
            so = masked(dot(kn[0:q0, :], qt) * SCALE_LOG2E, start, 0, q0, False)
            top = jnp.maximum(top, jnp.max(so, axis=0, keepdims=True))
        pd = jnp.exp2(sd - top)
        total = jnp.sum(pd, axis=0, keepdims=True)
        out = dot(vt[:, q0 : q0 + QB], pd.astype(bf16))
        if i:
            po = jnp.exp2(so - top)
            total = total + jnp.sum(po, axis=0, keepdims=True)
            out = out + dot(vt[:, 0:q0], po.astype(bf16))
        out = out / total
        ot[:, q0 : q0 + QB] = out
        lse[:, q0 : q0 + QB] = top + jnp.log2(total)
        low = out.astype(bf16)
        atts[2 * i] = low[:, 0:TOK]
        atts[2 * i + 1] = low[:, TOK:QB]
        after(2 * i)
        after(2 * i + 1)


def attend_backward(offs_ref, qk, vals, kn, kt, vn, qn, don, dor, ot, lse, dqkv, dk, dv, after):
    for s in range(NB):
        rows = slice(s * TOK, (s + 1) * TOK)
        vn[rows, :] = turned(vals[s])
        qn[rows, :] = turned(qk[s, 0:48, :])
        don[rows, :] = turned(dor[s])
        kt[:, rows] = qk[s, 48:96, :]
    last = SEQ // QB - 1
    for i in reversed(range(SEQ // QB)):
        q0 = i * QB
        qt = pair(qk, i, 0, 48)
        dot_t = pair(dor, i, 0, 48)
        start = segment_starts(offs_ref, q0, QB)
        level = lse[:, q0 : q0 + QB]
        inner = jnp.sum(dot_t.astype(f32) * ot[:, q0 : q0 + QB], axis=0, keepdims=True)
        q_n = qn[q0 : q0 + QB, :]
        do_n = don[q0 : q0 + QB, :]
        dq = None
        for a, b, diagonal in ([(0, q0, False)] if i else []) + [(q0, q0 + QB, True)]:
            scores = masked(dot(kn[a:b, :], qt) * SCALE_LOG2E, start, a, q0, diagonal)
            probs = jnp.exp2(scores - level)
            dp = dot(vn[a:b, :], dot_t)
            ds = (probs * (dp - inner)).astype(bf16)
            dv_part = dot(probs.astype(bf16), do_n)
            dk_part = dot(ds, q_n)
            if i == last:
                dk[a:b, :] = dk_part
                dv[a:b, :] = dv_part
            else:
                dk[a:b, :] += dk_part
                dv[a:b, :] += dv_part
            dq_part = dot(kt[:, a:b], ds)
            dq = dq_part if dq is None else dq + dq_part
        dq = (dq * SCALE).astype(bf16)
        for h in range(2):
            s = 2 * i + h
            rows = slice(s * TOK, (s + 1) * TOK)
            dqkv[s, 0:48, :] = dq[:, h * TOK : (h + 1) * TOK]
            dqkv[s, 48:96, :] = (jnp.transpose(dk[rows, :]) * SCALE).astype(bf16)
            dqkv[s, 96:144, :] = jnp.transpose(dv[rows, :]).astype(bf16)
        after(i)


def norm_parts(values):
    center = values - jnp.mean(values, axis=-1, keepdims=True)
    spread = jnp.mean(center * center, axis=-1, keepdims=True)
    rs = lax.rsqrt(spread + EPSILON)
    return center * rs, rs


def norm_back(grad, n, rs, gain):
    gg = grad * gain
    return rs * (
        gg - jnp.mean(gg, axis=-1, keepdims=True) - n * jnp.mean(gg * n, axis=-1, keepdims=True)
    )


def over_tokens(values):
    return jnp.sum(values, axis=0, keepdims=True)


ORDERS = (("x", "y", "z"), ("y", "z", "x"), ("z", "x", "y"))


class Sums:
    def __init__(self, group, ag, near, buf2, recv2, recv3, buf4, send, recv, own):
        self.group, self.ag, self.near = group, ag, near
        self.buf2, self.recv2, self.recv3, self.buf4 = buf2, recv2, recv3, buf4
        self.send, self.recv, self.own = send, recv, own
        self.core = lax.rem(lax.axis_index("rows"), 2)
        self.place = [[axis_place(a) for a in order] for order in ORDERS]
        keys = [(g, p) for g in range(3) for p in range(3)]
        self.live = {key: [] for key in keys}
        self.later = {key: [] for key in keys}
        self.used = {key: 0 for key in keys}
        self.mine = {}
        self.at = [0, 0, 0]
        self.sent = []
        self.shared = []
        self.stages = [
            self.near_first, self.near_second, self.across, self.third,
            self.back_across, self.back_near, self.back_far, self.back_last,
        ]

    def go(self, g, p, src, dst, device):
        n = self.used[g, p]
        self.used[g, p] = n + 1
        copy = remote(src, dst, self.send.at[g, p, n], self.recv.at[g, p, n], device)
        copy.start()
        self.sent.append(copy)
        return copy

    def step(self, *groups):
        for g in groups:
            k = self.at[g]
            if k >= len(self.stages):
                continue
            self.at[g] = k + 1
            for p in range(3):
                for copy in self.live[g, p]:
                    copy.wait_recv()
                self.live[g, p] = self.stages[k](g, p)

    def end(self):
        while min(self.at) < len(self.stages):
            self.step(*[g for g in (2, 0, 1) if self.at[g] == min(self.at)])
        for copies in self.live.values():
            for copy in copies:
                copy.wait_recv()
        for copy in self.shared:
            copy.wait_recv()
        for copy in self.sent:
            copy.wait_send()

    def there(self, p, axis, j):
        return lax.rem(self.place[p][axis] + j, 4)

    def ends(self, p):
        return axis_peer(ORDERS[p][0], 1), axis_peer(ORDERS[p][0], 3)

    def block(self, g, p, j, lo, size):
        quarter = GROUP_ROWS[g] // 12
        return pl.ds(p * quarter * 4 + self.there(p, 0, j) * quarter + lo, size)

    def near_first(self, g, p):
        right, left = self.ends(p)
        group, near = self.group[g], self.near[g]
        quarter = GROUP_ROWS[g] // 12
        half = quarter // 2
        first = [
            self.go(g, p, group.at[self.block(g, p, 2, 0, half)], near.at[p, pl.ds(0, half)], right),
            self.go(g, p, group.at[self.block(g, p, 2, half, half)], near.at[p, pl.ds(half, half)], left),
        ]
        self.later[g, p] = [
            self.go(g, p, group.at[self.block(g, p, 1, half, half)], near.at[p, pl.ds(quarter + half, half)], right),
            self.go(g, p, group.at[self.block(g, p, 3, 0, half)], near.at[p, pl.ds(2 * quarter, half)], left),
        ]
        return first

    def near_second(self, g, p):
        right, left = self.ends(p)
        group, near = self.group[g], self.near[g]
        quarter = GROUP_ROWS[g] // 12
        half = quarter // 2
        copies = []
        for j, lo, device in ((1, 0, right), (3, half, left)):
            rows = self.block(g, p, j, lo, half)
            both = group[rows].astype(f32) + near[p, lo : lo + half].astype(f32)
            group[rows] = both.astype(bf16)
            spot = near.at[p, pl.ds((quarter if j == 1 else 2 * quarter) + lo, half)]
            copies.append(self.go(g, p, group.at[rows], spot, device))
        return copies + self.later[g, p]

    def fan(self, g, p, axis, pick):
        copies = []
        for j in range(1, 4):
            src, dst = pick(j, self.there(p, axis, j))
            copies.append(self.go(g, p, src, dst, axis_peer(ORDERS[p][axis], j)))
        return copies

    def across(self, g, p):
        quarter = GROUP_ROWS[g] // 12
        size = quarter // 4
        near, buf2, recv2 = self.near[g], self.buf2[g], self.recv2[g]
        mine = self.group[g][self.block(g, p, 0, 0, quarter)].astype(f32)
        mine = mine + near[p, quarter : 2 * quarter].astype(f32) + near[p, 2 * quarter : 3 * quarter].astype(f32)
        buf2[p] = mine.astype(bf16)
        return self.fan(g, p, 1, lambda j, q: (buf2.at[p, pl.ds(q * size, size)], recv2.at[p, j - 1]))

    def third(self, g, p):
        size = GROUP_ROWS[g] // 48
        recv2, recv3 = self.recv2[g], self.recv3[g]
        acc = self.buf2[g][p, pl.ds(self.place[p][1] * size, size)].astype(f32)
        for j in range(3):
            acc = acc + recv2[p, j].astype(f32)
        here = self.place[p][2]
        recv3[p, here] = acc.astype(bf16)
        return self.fan(g, p, 2, lambda j, q: (recv3.at[p, here], recv3.at[p, here]))

    def spot(self, g, p, lo, size):
        base = sum(GROUP_ROWS[:g]) + p * (GROUP_ROWS[g] // 3)
        return self.ag.at[self.core, pl.ds(base + lo, size)]

    def back_across(self, g, p):
        size = GROUP_ROWS[g] // 48
        recv3, buf4 = self.recv3[g], self.buf4[g]
        acc = recv3[p, 0].astype(f32)
        for j in range(1, 4):
            acc = acc + recv3[p, j].astype(f32)
        buf4[p] = acc.astype(bf16)
        spot = self.spot(g, p, (self.place[p][0] * 4 + self.place[p][1]) * size, size)
        copies = self.fan(g, p, 1, lambda j, q: (buf4.at[p], spot))
        self.mine[g, p] = pltpu.make_async_copy(buf4.at[p], spot, self.own.at[g, p])
        self.mine[g, p].start()
        return copies

    def whole(self, g, p, j, lo=0, size=None):
        quarter = GROUP_ROWS[g] // 12
        return self.spot(g, p, self.there(p, 0, j) * quarter + lo, size or quarter)

    def share(self, g, p, j):
        spot = self.whole(g, p, j)
        self.shared.append(self.go(g, p, spot, spot, sibling()))

    def back_near(self, g, p):
        self.mine[g, p].wait()
        right, left = self.ends(p)
        spot = self.whole(g, p, 0)
        copies = [self.go(g, p, spot, spot, right), self.go(g, p, spot, spot, left)]
        self.share(g, p, 0)
        return copies

    def back_far(self, g, p):
        right, left = self.ends(p)
        half = GROUP_ROWS[g] // 24
        low = self.whole(g, p, 3, 0, half)
        high = self.whole(g, p, 1, half, half)
        copies = [self.go(g, p, low, low, right), self.go(g, p, high, high, left)]
        self.share(g, p, 1)
        self.share(g, p, 3)
        return copies

    def back_last(self, g, p):
        self.share(g, p, 2)
        return []


def exchange(src, dst, send, recv):
    r = lax.axis_index("rows")
    s = lax.axis_index("seq")
    copies = []
    for d in range(1, 16):
        peer = seq_peer(d)
        copy = remote(src.at[peer], dst.at[s], send.at[d], recv.at[d], (r, peer))
        copy.start()
        copies.append(copy)
    dst[s] = src[s]
    return copies


def hand_on(src, dst, send, recv, block):
    r = lax.axis_index("rows")
    s = lax.axis_index("seq")
    d = lax.rem(block - s + 16, 16)

    @pl.when(s != block)
    def _():
        remote(src.at[block], dst.at[s], send.at[d], recv.at[d], (r, block)).start()

    @pl.when(s == block)
    def _():
        dst[s] = src[block]


def handed(src, dst, send, recv):
    r = lax.axis_index("rows")
    s = lax.axis_index("seq")
    return [remote(src.at[0], dst.at[s], send.at[d], recv.at[d], (r, seq_peer(d))) for d in range(1, 16)]


class Vectors:
    def __init__(self, buf, slots, send_sem, recv_sem):
        self.buf, self.slots, self.send_sem, self.recv_sem = buf, slots, send_sem, recv_sem
        self.at = 0
        self.live = []

    def step(self):
        k = self.at
        self.at = k + 1
        for copy in self.live:
            copy.wait()
        self.live = []
        if k == 0:
            value = self.buf[0]
        else:
            value = self.slots[k - 1, 0]
            for j in range(1, 4 if k < 4 else 2):
                value = value + self.slots[k - 1, j]
        if k == 4:
            self.buf[1] = value
            return
        here = axis_place("xyz"[k]) if k < 3 else lax.rem(lax.axis_index("rows"), 2)
        devices = [axis_peer("xyz"[k], j) for j in range(1, 4)] if k < 3 else [sibling()]
        self.slots[k, here] = value
        for j, device in enumerate(devices):
            spot = self.slots.at[k, here]
            copy = remote(spot, spot, self.send_sem.at[k, j], self.recv_sem.at[k, j], device)
            copy.start()
            self.live.append(copy)


def block_kernel(
    offs_h, x_h, dy_h, ln1g_h, ln1b_h, bq_h, bv_h, bout_h, ln2g_h, ln2b_h, bup_h, bdown_h,
    wqkv_h, wout_h, wup_h, wdown_h,
    out_h, ig_h, ag, vecs_h,
    offs, x_ref, dy_ref, ln1g, ln1b, bq, bv, bout, ln2g, ln2b, bup, bdown,
    out_ref, ig_ref, vecs,
    wqkv, wout, wup, wdown, wsem,
    qkt, vals, rqk, rv, kn, vt, ot, lse, atts, ratt,
    h1t, h1ts, n1, rs1, h2t, h2ts, dys, actt, actts, gp, gps, gb, gbs, attts, gres,
    gattt, rda, kt, vn, qn, don, dk, dv, dqkv, rdq, dqs,
    asend, arecv, ssend, srecv,
    *rest,
):
    group, near, buf2, recv2, recv3, buf4 = [rest[3 * k : 3 * k + 3] for k in range(6)]
    (gsend, grecv, gown, vbuf, vrecv, vsend, vrsem, lbuf, lrecv, lsend, lrsem, osem) = rest[18:]
    loads = {}

    def load(name, src, dst):
        copy = pltpu.make_async_copy(src, dst, wsem.at[len(loads)])
        copy.start()
        loads[name] = copy

    load("x", x_h, x_ref)
    load("ln1g", ln1g_h, ln1g)
    load("ln1b", ln1b_h, ln1b)
    for t in (1, 0, 2):
        cols = pl.ds(t * D, D)
        load(f"qkv{t}", wqkv_h.at[:, cols], wqkv.at[:, cols])
    load("bq", bq_h, bq)
    load("bv", bv_h, bv)
    load("dy", dy_h, dy_ref)
    load("offs", offs_h, offs)
    load("out", wout_h, wout)
    for name, src, dst in (
        ("bout", bout_h, bout), ("ln2g", ln2g_h, ln2g), ("ln2b", ln2b_h, ln2b),
        ("bup", bup_h, bup), ("bdown", bdown_h, bdown),
    ):
        load(name, src, dst)
    load("up", wup_h, wup)
    load("down", wdown_h, wdown)
    stores = []

    def ready(*names):
        for name in names:
            loads[name].wait()

    def store(src, dst):
        copy = pltpu.make_async_copy(src, dst, osem.at[len(stores)])
        copy.start()
        stores.append(copy)

    bar, count = greet(True, ("y",))
    vecg = vbuf.at[0]
    vecl = lbuf.at[0]
    early = Vectors(vbuf, vrecv, vsend, vrsem)
    late = Vectors(lbuf, lrecv, lsend, lrsem)
    sums = Sums(group, ag, near, buf2, recv2, recv3, buf4, gsend, grecv, gown)

    def line(ref):
        return ref[...].astype(f32).reshape(1, D)

    core = lax.rem(lax.axis_index("rows"), 2)
    other = 1 - core
    sib = sibling()
    to_sib = []

    def send_sib(n, src, dst):
        copy = remote(src, dst, ssend.at[n], srecv.at[n], sib)
        copy.start()
        to_sib.append(copy)

    ready("x", "ln1g", "ln1b")
    x = x_ref[...].astype(f32)
    n, rs = norm_parts(x)
    n1[...] = n
    rs1[...] = rs
    h1f = n * line(ln1g) + line(ln1b)
    h1 = h1f.astype(bf16)
    h1t[...] = jnp.transpose(h1f).astype(bf16)
    for t in (1, 0, 2):
        ready(f"qkv{t}")
        y = dot(h1, wqkv[:, t * D : (t + 1) * D])
        if t == 0:
            ready("bq")
            y = y + line(bq)
        if t == 2:
            ready("bv")
            y = y + line(bv)
        low = jnp.transpose(y).astype(bf16).reshape(H, HS, TOK)
        if t < 2:
            qkt[:, t * HS : (t + 1) * HS, :] = low
        else:
            vals[...] = low
        if t == 0:
            pl.semaphore_wait(bar, count)
            moved = exchange(qkt, rqk, asend.at[0], arecv.at[0])
    moved += exchange(vals, rv, asend.at[1], arecv.at[1])
    send_sib(0, h1t, h1ts)
    ready("dy", "offs")
    send_sib(1, dy_ref, dys)
    for copy in moved:
        copy.wait()

    attend_forward(
        offs, rqk, rv, kn, vt, ot, lse, atts,
        lambda block: hand_on(atts, ratt, asend.at[2], arecv.at[2], block),
    )
    moved = handed(atts, ratt, asend.at[2], arecv.at[2])
    ready("out", "bout", "ln2g", "ln2b", "bup", "bdown", "up", "down")
    for copy in moved:
        copy.wait()

    att = jnp.transpose(ratt[...].reshape(D, TOK).astype(f32)).astype(bf16)
    send_sib(2, ratt.at[pl.ds(other * 8, 8)], attts)
    resid = x_ref[...].astype(f32) + dot(att, wout[...]) + line(bout)
    n2, rs2 = norm_parts(resid)
    h2f = n2 * line(ln2g) + line(ln2b)
    h2 = h2f.astype(bf16)
    h2t[...] = jnp.transpose(h2f).astype(bf16)
    send_sib(3, h2t, h2ts)
    dy = dy_ref[...]
    down = None
    dh2 = None
    for c in range(4):
        cols = slice(c * D, (c + 1) * D)
        pre = dot(h2, wup[:, cols]) + bup[cols].astype(f32).reshape(1, D)
        square = pre * pre
        t = jnp.tanh(GELU_C * (pre + GELU_A * (square * pre)))
        act = 0.5 * pre * (1.0 + t)
        slope = 0.5 * (1.0 + t) + (0.5 * GELU_C) * pre * (1.0 - t * t) * (1.0 + (3.0 * GELU_A) * square)
        part = dot(act.astype(bf16), wdown[cols, :])
        down = part if down is None else down + part
        actt[c] = jnp.transpose(act).astype(bf16)
        gpre = (dot_nt(dy, wdown[cols, :]) * slope).astype(bf16)
        gp[c] = gpre
        vecg[BUP + c : BUP + c + 1, :] = over_tokens(gpre.astype(f32))
        part = dot_nt(gpre, wup[:, cols])
        dh2 = part if dh2 is None else dh2 + part
    send_sib(4, actt.at[pl.ds(other * 2, 2)], actts)
    send_sib(5, gp.at[pl.ds(other * 2, 2)], gps)
    out_ref[...] = (resid + down + line(bdown)).astype(bf16)
    store(out_ref, out_h)
    vecg[BDOWN : BDOWN + 1, :] = over_tokens(dy.astype(f32))
    vecg[LN2G : LN2G + 1, :] = over_tokens(dh2 * n2)
    vecg[LN2B : LN2B + 1, :] = over_tokens(dh2)
    grad = dy.astype(f32) + norm_back(dh2, n2, rs2, line(ln2g))
    gres[...] = grad
    branch = grad.astype(bf16)
    gb[...] = branch
    vecg[BOUT : BOUT + 1, :] = over_tokens(branch.astype(f32))
    early.step()
    gattt[...] = jnp.transpose(dot_nt(branch, wout[...])).astype(bf16).reshape(H, HS, TOK)
    moved = exchange(gattt, rda, asend.at[3], arecv.at[3])
    send_sib(6, gb, gbs)

    for k in (1, 2, 3, 4, 5, 6):
        to_sib[k].wait()
    dy2 = jnp.concatenate([dy, dys[...]], axis=0)
    for j in range(2):
        left = jnp.concatenate([actt[core * 2 + j], actts[j]], axis=1)
        res = dot(left, dy2).astype(bf16)
        for t in range(6):
            lo = t * 1536 + j * D
            group[0][lo : lo + D, :] = res[:, t * TOK : (t + 1) * TOK]
    sums.step(0)
    left = jnp.concatenate([h2t[...], h2ts[...]], axis=1)
    for j in range(2):
        right = jnp.concatenate([gp[core * 2 + j], gps[j]], axis=0)
        res = dot(left, right).astype(bf16)
        for t in range(6):
            lo = (j * 6 + t) * D
            group[1][lo : lo + D, :] = res[:, t * TOK : (t + 1) * TOK]
    left = jnp.concatenate(
        [ratt[pl.ds(core * 8, 8)].reshape(384, TOK), attts[...].reshape(384, TOK)], axis=1
    )
    right = jnp.concatenate([gb[...], gbs[...]], axis=0)
    res = dot(left, right).astype(bf16)
    for t in range(6):
        lo = OUT_ROW + t * 384
        group[1][lo : lo + 384, :] = res[:, t * TOK : (t + 1) * TOK]
    sums.step(1)

    for copy in moved:
        copy.wait()
    def between(i):
        for half in (0, 1):
            hand_on(dqkv, rdq, asend.at[4], arecv.at[4], 2 * i + half)
        if i == 4:
            early.step()

    attend_backward(offs, rqk, rv, kn, kt, vn, qn, don, rda, ot, lse, dqkv, dk, dv, between)
    sums.step(0)
    early.step()
    sums.step(1)
    for copy in handed(dqkv, rdq, asend.at[4], arecv.at[4]):
        copy.wait()
    send_sib(7, rdq.at[pl.ds(other * 8, 8)], dqs)

    dh1t = None
    ones = jnp.ones((8, TOK), bf16)
    for t in range(3):
        grad_t = rdq[:, t * HS : (t + 1) * HS, :].reshape(D, TOK)
        part = dot(wqkv[:, t * D : (t + 1) * D], grad_t)
        dh1t = part if dh1t is None else dh1t + part
        if t != 1:
            row = BQ if t == 0 else BV
            vecl[row : row + 1, :] = dot_nt(ones, grad_t)[0:1, :]
    to_sib[0].wait()
    to_sib[7].wait()
    left = jnp.concatenate([h1t[...], h1ts[...]], axis=1)
    for t in range(3):
        mine = rdq[pl.ds(core * 8, 8), t * HS : (t + 1) * HS, :].reshape(384, TOK)
        theirs = dqs[:, t * HS : (t + 1) * HS, :].reshape(384, TOK)
        res = dot_nt(left, jnp.concatenate([mine, theirs], axis=1)).astype(bf16)
        for u in range(3):
            lo = (t * 3 + u) * D
            group[2][lo : lo + D, :] = res[:, u * TOK : (u + 1) * TOK]
    sums.step(2)

    dh1 = jnp.transpose(dh1t)
    n = n1[...]
    vecl[LN1G : LN1G + 1, :] = over_tokens(dh1 * n)
    vecl[LN1B : LN1B + 1, :] = over_tokens(dh1)
    vecl[4:8, :] = jnp.zeros((4, D), f32)
    late.step()
    ig_ref[...] = (gres[...] + norm_back(dh1, n, rs1[...], line(ln1g))).astype(bf16)
    store(ig_ref, ig_h)
    early.step()

    sums.step(0, 2)
    late.step()
    sums.step(1, 2)
    late.step()
    early.step()
    vecs[0] = vbuf[1]
    sums.step(0, 2)
    late.step()
    sums.step(1, 0, 2)
    late.step()
    vecs[1] = lbuf[1]
    store(vecs, vecs_h)
    sums.step(1, 0, 2)
    sums.step(1, 0, 2)
    sums.end()
    for copy in stores:
        copy.wait()


VMEM = pl.BlockSpec(memory_space=pltpu.VMEM)
SMEM = pl.BlockSpec(memory_space=pltpu.SMEM)
ANY = pl.BlockSpec(memory_space=pl.ANY)


def call_block(offsets, x, dy, vectors, weights):
    v = pltpu.VMEM
    dma = pltpu.SemaphoreType.DMA
    shape = jax.ShapeDtypeStruct
    return pl.pallas_call(
        block_kernel,
        out_shape=(
            shape((TOK, D), bf16),
            shape((TOK, D), bf16),
            shape((2, ALL_ROWS, TOK), bf16),
            shape((2, VROWS, D), f32),
        ),
        in_specs=[ANY] * 16,
        out_specs=(ANY, ANY, ANY, ANY),
        scratch_shapes=[
            pltpu.SMEM((1, 8), jnp.int32), v((TOK, D), bf16), v((TOK, D), bf16),
            *[v((FF if k == 7 else D,), bf16) for k in range(9)],
            v((TOK, D), bf16), v((TOK, D), bf16), v((2, VROWS, D), f32),
            v((D, 3 * D), bf16), v((D, D), bf16), v((D, FF), bf16), v((FF, D), bf16), dma((20,)),
            v((NB, 96, TOK), bf16), v((NB, HS, TOK), bf16), v((NB, 96, TOK), bf16), v((NB, HS, TOK), bf16),
            v((SEQ, HS), bf16), v((HS, SEQ), bf16),
            v((HS, SEQ), f32), v((1, SEQ), f32), v((NB, HS, TOK), bf16), v((NB, HS, TOK), bf16),
            v((D, TOK), bf16), v((D, TOK), bf16), v((TOK, D), f32), v((TOK, 1), f32),
            v((D, TOK), bf16), v((D, TOK), bf16), v((TOK, D), bf16),
            v((4, D, TOK), bf16), v((2, D, TOK), bf16), v((4, TOK, D), bf16), v((2, TOK, D), bf16),
            v((TOK, D), bf16), v((TOK, D), bf16), v((8, HS, TOK), bf16), v((TOK, D), f32),
            v((NB, HS, TOK), bf16), v((NB, HS, TOK), bf16),
            v((HS, SEQ), bf16), v((SEQ, HS), bf16), v((SEQ, HS), bf16), v((SEQ, HS), bf16),
            v((SEQ, HS), f32), v((SEQ, HS), f32),
            v((NB, 144, TOK), bf16), v((NB, 144, TOK), bf16), v((8, 144, TOK), bf16),
            dma((5, 16)), dma((5, 16)), dma((8,)), dma((8,)),
            *[v((r, TOK), bf16) for r in GROUP_ROWS],
            *[v((3, r // 4, TOK), bf16) for r in GROUP_ROWS],
            *[v((3, r // 12, TOK), bf16) for r in GROUP_ROWS],
            *[v((3, 3, r // 48, TOK), bf16) for r in GROUP_ROWS],
            *[v((3, 4, r // 48, TOK), bf16) for r in GROUP_ROWS],
            *[v((3, r // 48, TOK), bf16) for r in GROUP_ROWS],
            dma((3, 3, 23)), dma((3, 3, 23)), dma((3, 3)),
            v((2, VROWS, D), f32), v((4, 4, VROWS, D), f32), dma((4, 3)), dma((4, 3)),
            v((2, VROWS, D), f32), v((4, 4, VROWS, D), f32), dma((4, 3)), dma((4, 3)), dma((3,)),
        ],
        compiler_params=pltpu.CompilerParams(
            collective_id=1, has_side_effects=True, vmem_limit_bytes=58 * 2**20
        ),
    )(offsets, x, dy, *vectors, *weights)


def widen_kernel(ag, vecs_h, done_h, ig_h, wqkv, wout, wup, wdown, out_h, grad_h, *rest):
    small_h, small, (vecs, inb, outb, isem, osem, vsem, ssem) = rest[:9], rest[9:18], rest[18:]
    passed = [
        pltpu.make_async_copy(done_h, out_h, vsem.at[0]),
        pltpu.make_async_copy(ig_h, grad_h, vsem.at[1]),
    ]
    for copy in passed:
        copy.start()
    fetch = pltpu.make_async_copy(vecs_h, vecs, vsem.at[2])
    fetch.start()

    def narrow():
        fetch.wait()
        fill()
        for k in range(9):
            copy = pltpu.make_async_copy(small[k], small_h[k], ssem.at[k])
            copy.start()
            passed.append(copy)

    def fill():
        places = ((1, LN1G), (1, LN1B), (1, BQ), (1, BV), (0, BOUT), (0, LN2G), (0, LN2B), (0, BUP), (0, BDOWN))
        for ref, (k, row) in zip(small, places):
            if row == BUP:
                for c in range(4):
                    ref[c * D : (c + 1) * D] = vecs[0, BUP + c : BUP + c + 1, :].reshape(D)
            else:
                ref[...] = vecs[k, row : row + 1, :].reshape(D)

    tasks = []
    for c in range(2):
        for j in range(2):
            for h in range(2):
                rows = [(h * 3 + t) * 1536 + j * D for t in range(3)]
                tasks.append((c, rows, wdown.at[pl.ds(c * 1536 + j * D, D), pl.ds(h * 384, 384)]))
        for h in range(4):
            rows = [GROUP_ROWS[0] + (h * 3 + t) * D for t in range(3)]
            tasks.append((c, rows, wup.at[:, pl.ds(c * 1536 + h * 384, 384)]))
        for h in range(3):
            rows = [GROUP_ROWS[0] + GROUP_ROWS[1] + (h * 3 + t) * D for t in range(3)]
            tasks.append((c, rows, wqkv.at[:, pl.ds(h * D + c * 384, 384)]))
        for h in range(2):
            rows = [GROUP_ROWS[0] + OUT_ROW + (h * 3 + t) * 384 for t in range(3)]
            tasks.append((c, rows, wout.at[pl.ds(c * 384, 384), pl.ds(h * 384, 384)]))
    slots = WIDEN_SLOTS

    def height(k):
        return 384 if tasks[k][2].shape[0] == 384 else D

    def load(k):
        c, rows, _ = tasks[k]
        size = height(k)
        for t, lo in enumerate(rows):
            pltpu.make_async_copy(
                ag.at[c, pl.ds(lo, size)], inb.at[k % slots, t, pl.ds(0, size)], isem.at[k % slots, t]
            ).start()

    def load_wait(k):
        c, rows, _ = tasks[k]
        size = height(k)
        for t, lo in enumerate(rows):
            pltpu.make_async_copy(
                ag.at[c, pl.ds(lo, size)], inb.at[k % slots, t, pl.ds(0, size)], isem.at[k % slots, t]
            ).wait()

    def store(k):
        return pltpu.make_async_copy(
            outb.at[k % slots, pl.ds(0, height(k))], tasks[k][2], osem.at[k % slots]
        )

    for k in range(slots - 1):
        load(k)
    narrow()
    for k in range(len(tasks)):
        if k + slots - 1 < len(tasks):
            load(k + slots - 1)
        load_wait(k)
        if k >= slots:
            store(k - slots).wait()
        size = height(k)
        for t in range(3):
            outb[k % slots, 0:size, t * TOK : (t + 1) * TOK] = inb[k % slots, t, 0:size, :].astype(f32)
        store(k).start()
    for k in range(len(tasks) - slots, len(tasks)):
        store(k).wait()
    for copy in passed:
        copy.wait()


def call_widen(ag, vecs, out, ig):
    v = pltpu.VMEM
    dma = pltpu.SemaphoreType.DMA
    shape = jax.ShapeDtypeStruct
    return pl.pallas_call(
        widen_kernel,
        out_shape=(
            shape((D, 3 * D), f32), shape((D, D), f32), shape((D, FF), f32), shape((FF, D), f32),
            shape((TOK, D), bf16), shape((TOK, D), bf16),
        ) + tuple(shape((FF if k == 7 else D,), f32) for k in range(9)),
        in_specs=[ANY] * 4,
        out_specs=(ANY,) * 15,
        scratch_shapes=[
            *[v((FF if k == 7 else D,), f32) for k in range(9)], v((2, VROWS, D), f32),
            v((WIDEN_SLOTS, 3, D, TOK), bf16), v((WIDEN_SLOTS, D, 384), f32), dma((WIDEN_SLOTS, 3)), dma((WIDEN_SLOTS,)),
            dma((3,)), dma((9,)),
        ],
        compiler_params=pltpu.CompilerParams(vmem_limit_bytes=58 * 2**20),
    )(ag, vecs, out, ig)


def local(
    block_input, offsets, ln1_gain, ln1_bias, w_qkv, bias_query, bias_value, w_out, bias_out,
    ln2_gain, ln2_bias, w_up, bias_up, w_down, bias_down, cotangent,
):
    out, ig, ag, vecs = call_block(
        offsets, block_input.reshape(TOK, D), cotangent.reshape(TOK, D),
        (ln1_gain, ln1_bias, bias_query, bias_value, bias_out, ln2_gain, ln2_bias, bias_up, bias_down),
        (w_qkv, w_out, w_up, w_down),
    )
    wide = call_widen(ag, vecs, out, ig)
    g_qkv, g_out, g_up, g_down, out, ig = wide[:6]
    s = wide[6:]
    return (
        out.reshape(1, TOK, D), ig.reshape(1, TOK, D),
        s[0], s[1], g_qkv, s[2], s[3], g_out, s[4], s[5], s[6], g_up, s[7], g_down, s[8],
    )


def solution(mesh):
    tokens = P("rows", "seq", None)
    return jax.shard_map(
        local,
        mesh=mesh,
        in_specs=(tokens, P("rows", None)) + (P(),) * 13 + (tokens,),
        out_specs=(tokens, tokens) + (P(),) * 13,
        check_vma=False,
    )
```

time: 197 us -> 134 us (0.68)
  Pallas kernels: 176 us -> 132 us
  local copies, waits for them, and re-layouts: 15.4 us -> 0 us
  other arithmetic: 4.84 us -> 0 us
    pallas_call x1 -> x0, Pallas kernels: 92.3 us -> none  [call_sum(): pl.pallas_call(sum_kernel, out_shape=(shape((2, 3, HALF_ROWS, TOK), bf16)...]
    pallas_call x1, Pallas kernels: 60.9 us -> 117 us  [call_block(): pl.pallas_call(block_kernel, out_shape=(shape((TOK, D), bf16), shape((TOK...]
    unnamed x18 -> x0, local copies, waits for them, and re-layouts: 14 us -> none
    pallas_call x1, Pallas kernels: 22.5 us -> 15 us  [call_widen(): pl.pallas_call(widen_kernel, out_shape=(shape((D, 3 * D), f32), shape((D,...]
    pallas_call x8 -> x0, other arithmetic: 4.84 us -> none  [call_widen(): pl.pallas_call(widen_kernel, out_shape=(shape((D, 3 * D), f32), shape((D,...]
where the time goes in v2:
time: 134 us; the launch traced here: 133 us
  Pallas kernels  132 us (99%)
    pallas_call x1, Pallas kernels, call_block(): pl.pallas_call(block_kernel, out_shape=(shape((TOK, D), bf16), shape((TOK...  117 us
    pallas_call x1, Pallas kernels, call_widen(): pl.pallas_call(widen_kernel, out_shape=(shape((D, 3 * D), f32), shape((D,...  15 us

profile of v2, /device:TPU:1, one launch (start us, length us, event | category | flops | bytes accessed | tf_op | source)
XLA Modules:
  0.0 133.2 jit_solution(3442347582468044661)
XLA Ops:
  0.7 117.4 %shard_map.271 = (bf16[128,768]{1,0:T(8,128)(2,1)}, bf16[128,768]{1,0:T(8,128)(2,1)}, bf16[2,27648,128]{2,1,0:T(8,128)(2,1)}, f32[2,8,768]{2,1,0:T(8,128)}) custom-call(s32[1,8]{1,0:T(1,128)} %offs_h.1, bf16[128,768]{1,0:T(8,128)(2,1)} %bitcast.4, bf16[128,768]{1,0:T(8,128)(2,1)} %bitcast.5, bf16[768]{0:T(1024)(128)(2,1)} %ln1g_h.1, bf16[768]{0:T(1024)(128)(2,1)} %ln1b_h.1, ...), custom_call_target="tpu_custom_call" | custom-call | tf_op jit(solution)/shard_map/pallas_call | solution.py:705
  118.1 15.0 %shard_map.272 = (f32[768,2304]{1,0:T(8,128)}, f32[768,768]{1,0:T(8,128)}, f32[768,3072]{1,0:T(8,128)}, f32[3072,768]{1,0:T(8,128)}, bf16[128,768]{1,0:T(8,128)(...) custom-call(bf16[2,27648,128]{2,1,0:T(8,128)(2,1)} %get-tuple-elemen, ...), custom_call_target="tpu_custom_call" | custom-call | tf_op jit(solution)/shard_map/pallas_call | solution.py:840

commit v3 on v2

v3 whole, which is shorter than its diff:
```python
import functools

import jax
import jax.numpy as jnp
from jax import lax
from jax.experimental import pallas as pl
from jax.experimental.pallas import tpu as pltpu
from jax.sharding import PartitionSpec as P

MESH = pl.DeviceIdType.MESH
f32 = jnp.float32
bf16 = jnp.bfloat16

D = 768
H = 16
FF = 3072
HS = 48
SEQ = 2048
TOK = 128
NB = 16
QB = 256
CUT_DOWN = (80, 64)
CUT_UP = (80, 64)
CUT_OUT = (32, 16)
SHARE = 112
HEAD_ROWS = 4 * SHARE
ROWS_LAST = SHARE + sum(CUT_OUT)
WAYS_DOWN = ((0, 48, "xzy"), (48, 48, "zyx"), (96, 48, "yxz"))
WAYS_UP = WAYS_DOWN
WAYS_LAST = ((0, 64, "xzy"), (64, 48, "zyx"), (112, 48, "yxz"))
SCALE = HS**-0.5
SCALE_LOG2E = SCALE * 1.4426950408889634
NEGATIVE = -1e30
EPSILON = 1e-05
GELU_C = 0.7978845608028654
GELU_A = 0.044715

LN1G, LN1B, BQ, BV = 0, 1, 2, 3
BOUT, LN2G, LN2B, BDOWN, BUP = 0, 1, 2, 3, 4
VROWS = 8
WIDEN_SLOTS = 6


def dot(a, b):
    return jnp.dot(a, b, preferred_element_type=f32)


def dot_nt(a, b):
    return lax.dot_general(a, b, (((1,), (1,)), ((), ())), preferred_element_type=f32)


def turned(block):
    return jnp.transpose(block.astype(f32)).astype(bf16)


def coords():
    r = lax.axis_index("rows")
    s = lax.axis_index("seq")
    return lax.div(r, 2), lax.rem(r, 2), lax.div(s, 4), lax.rem(s, 4)


def device_at(y, c, z, x):
    return (y * 2 + c, z * 4 + x)


def remote(src, dst, send, recv, device):
    return pltpu.make_async_remote_copy(
        src_ref=src, dst_ref=dst, send_sem=send, recv_sem=recv, device_id=device, device_id_type=MESH
    )


def seq_peer(d):
    s = lax.axis_index("seq")
    return lax.rem(s + d, 16)


def axis_peer(axis, j):
    y, c, z, x = coords()
    if axis == "y":
        y = lax.rem(y + j, 4)
    elif axis == "z":
        z = lax.rem(z + j, 4)
    else:
        x = lax.rem(x + j, 4)
    return device_at(y, c, z, x)


def axis_place(axis):
    y, c, z, x = coords()
    return {"y": y, "z": z, "x": x}[axis]


def sibling():
    y, c, z, x = coords()
    return device_at(y, 1 - c, z, x)


def greet():
    bar = pltpu.get_barrier_semaphore()
    r = lax.axis_index("rows")
    s = lax.axis_index("seq")
    devices = [(r, seq_peer(d)) for d in range(1, 16)] + [(lax.rem(r + d, 8), s) for d in range(1, 8)]
    for device in devices:
        pl.semaphore_signal(bar, inc=1, device_id=device, device_id_type=MESH)
    return bar, len(devices)


def masked(scores, start, key0, query0, diagonal):
    key = lax.broadcasted_iota(jnp.int32, scores.shape, 0) + key0
    ok = key >= start
    if diagonal:
        query = lax.broadcasted_iota(jnp.int32, scores.shape, 1) + query0
        ok = ok & (key <= query)
    return jnp.where(ok, scores, NEGATIVE)


def segment_starts(offs_ref, query0, count):
    place = lax.broadcasted_iota(jnp.int32, (1, count), 1) + query0
    start = jnp.zeros((1, count), jnp.int32)
    for j in range(8):
        o = offs_ref[0, j]
        start = jnp.where(place >= o, o, start)
    return start


def pair(ref, i, lo, hi):
    return jnp.concatenate([ref[2 * i, lo:hi, :], ref[2 * i + 1, lo:hi, :]], axis=1)


def attend_forward(offs_ref, qk, vals, kn, vt, ot, lse, atts, after):
    for s in range(NB):
        kn[s * TOK : (s + 1) * TOK, :] = turned(qk[s, 48:96, :])
        vt[:, s * TOK : (s + 1) * TOK] = vals[s]
    for i in range(SEQ // QB):
        q0 = i * QB
        qt = pair(qk, i, 0, 48)
        start = segment_starts(offs_ref, q0, QB)
        sd = masked(dot(kn[q0 : q0 + QB, :], qt) * SCALE_LOG2E, start, q0, q0, True)
        top = jnp.max(sd, axis=0, keepdims=True)
        if i:
            so = masked(dot(kn[0:q0, :], qt) * SCALE_LOG2E, start, 0, q0, False)
            top = jnp.maximum(top, jnp.max(so, axis=0, keepdims=True))
        pd = jnp.exp2(sd - top)
        total = jnp.sum(pd, axis=0, keepdims=True)
        out = dot(vt[:, q0 : q0 + QB], pd.astype(bf16))
        if i:
            po = jnp.exp2(so - top)
            total = total + jnp.sum(po, axis=0, keepdims=True)
            out = out + dot(vt[:, 0:q0], po.astype(bf16))
        out = out / total
        ot[:, q0 : q0 + QB] = out
        lse[:, q0 : q0 + QB] = top + jnp.log2(total)
        low = out.astype(bf16)
        atts[2 * i] = low[:, 0:TOK]
        atts[2 * i + 1] = low[:, TOK:QB]
        after(2 * i)
        after(2 * i + 1)


def attend_backward(offs_ref, qk, vals, kn, kt, vn, qn, don, dor, ot, lse, dqkv, dk, dv, after):
    for s in range(NB):
        rows = slice(s * TOK, (s + 1) * TOK)
        vn[rows, :] = turned(vals[s])
        qn[rows, :] = turned(qk[s, 0:48, :])
        don[rows, :] = turned(dor[s])
        kt[:, rows] = qk[s, 48:96, :]
    last = SEQ // QB - 1
    for i in reversed(range(SEQ // QB)):
        q0 = i * QB
        qt = pair(qk, i, 0, 48)
        dot_t = pair(dor, i, 0, 48)
        start = segment_starts(offs_ref, q0, QB)
        level = lse[:, q0 : q0 + QB]
        inner = jnp.sum(dot_t.astype(f32) * ot[:, q0 : q0 + QB], axis=0, keepdims=True)
        q_n = qn[q0 : q0 + QB, :]
        do_n = don[q0 : q0 + QB, :]
        dq = None
        for a, b, diagonal in ([(0, q0, False)] if i else []) + [(q0, q0 + QB, True)]:
            scores = masked(dot(kn[a:b, :], qt) * SCALE_LOG2E, start, a, q0, diagonal)
            probs = jnp.exp2(scores - level)
            dp = dot(vn[a:b, :], dot_t)
            ds = (probs * (dp - inner)).astype(bf16)
            dv_part = dot(probs.astype(bf16), do_n)
            dk_part = dot(ds, q_n)
            if i == last:
                dk[a:b, :] = dk_part
                dv[a:b, :] = dv_part
            else:
                dk[a:b, :] += dk_part
                dv[a:b, :] += dv_part
            dq_part = dot(kt[:, a:b], ds)
            dq = dq_part if dq is None else dq + dq_part
        dq = (dq * SCALE).astype(bf16)
        for h in range(2):
            s = 2 * i + h
            rows = slice(s * TOK, (s + 1) * TOK)
            dqkv[s, 0:48, :] = dq[:, h * TOK : (h + 1) * TOK]
            dqkv[s, 48:96, :] = (jnp.transpose(dk[rows, :]) * SCALE).astype(bf16)
            dqkv[s, 96:144, :] = jnp.transpose(dv[rows, :]).astype(bf16)
        after(i)


def norm_parts(values):
    center = values - jnp.mean(values, axis=-1, keepdims=True)
    spread = jnp.mean(center * center, axis=-1, keepdims=True)
    rs = lax.rsqrt(spread + EPSILON)
    return center * rs, rs


def norm_back(grad, n, rs, gain):
    gg = grad * gain
    return rs * (
        gg - jnp.mean(gg, axis=-1, keepdims=True) - n * jnp.mean(gg * n, axis=-1, keepdims=True)
    )


def over_tokens(values):
    return jnp.sum(values, axis=0, keepdims=True)


def arrived(gauge, sem):
    pltpu.make_async_copy(gauge, gauge, sem).wait()


class Steps:
    def __init__(self, send, recv):
        self.send, self.recv = send, recv
        self.sent = []
        self.live = []
        self.at = 0

    def go(self, group, src, dst, device):
        remote(src, dst, self.send.at[group], self.recv.at[group], device).start()

    def expect(self, group, gauge):
        self.live.append((group, gauge))
        self.sent.append((group, gauge))

    def collect(self):
        for group, gauge in self.live:
            arrived(gauge, self.recv.at[group])
        self.live = []

    def step(self):
        self.collect()
        k = self.at
        self.at = k + 1
        self.run(k)

    def done(self):
        for group, gauge in self.sent:
            arrived(gauge, self.send.at[group])
        self.sent = []


class Scatter(Steps):
    def __init__(self, cuts, parts, recv1, mid, recv2, share, send, recv):
        super().__init__(send, recv)
        self.cuts, self.parts, self.recv1, self.mid, self.recv2, self.share = cuts, parts, recv1, mid, recv2, share

    def put(self, value, offset):
        at, rows = 0, value.shape[0]
        while at < rows:
            k = 0 if offset < 16 * self.cuts[0] else 1
            inside = offset - k * 16 * self.cuts[0]
            block, lo = inside // self.cuts[k], inside % self.cuts[k]
            size = min(self.cuts[k] - lo, rows - at)
            self.parts[k][block // 4, block % 4, lo : lo + size, :] = value[at : at + size]
            at += size
            offset += size

    def run(self, k):
        z, x = axis_place("z"), axis_place("x")
        first, second = self.parts
        if k == 0:
            for j in range(1, 4):
                self.go(0, first.at[:, lax.rem(x + j, 4)], self.recv1[0].at[j - 1], axis_peer("x", j))
                self.go(1, second.at[lax.rem(z + j, 4)], self.recv1[1].at[j - 1], axis_peer("z", j))
            for n in range(2):
                self.expect(n, self.recv1[n])
        elif k == 1:
            for n, mine in enumerate((first[:, x], second[z])):
                acc = mine.astype(f32)
                for j in range(3):
                    acc = acc + self.recv1[n][j].astype(f32)
                self.mid[n][...] = acc.astype(bf16)
            for j in range(1, 4):
                self.go(2, self.mid[0].at[lax.rem(z + j, 4)], self.recv2[0].at[j - 1], axis_peer("z", j))
                self.go(3, self.mid[1].at[lax.rem(x + j, 4)], self.recv2[1].at[j - 1], axis_peer("x", j))
            for n in range(2):
                self.expect(2 + n, self.recv2[n])
        else:
            lo = 0
            for n, here in enumerate((z, x)):
                acc = self.mid[n][here].astype(f32)
                for j in range(3):
                    acc = acc + self.recv2[n][j].astype(f32)
                self.share[lo : lo + self.cuts[n], :] = acc.astype(bf16)
                lo += self.cuts[n]


class Spread(Steps):
    def __init__(self, share, ag, ways, send, recv, own):
        super().__init__(send, recv)
        self.share, self.ag, self.ways, self.own = share, ag, ways, own

    def spot(self, lo, size, whole, **at):
        core = lax.rem(lax.axis_index("rows"), 2)
        index = [at[a] if a in at else slice(None) if a in whole else axis_place(a) for a in "zxy"]
        return self.ag.at[(core, *index, pl.ds(lo, size))]

    def pass_on(self, spot):
        self.go(4, spot, spot, sibling())

    def run(self, k):
        ag = self.ag
        if k == 1:
            self.kept.wait()
        for lo, size, order in self.ways:
            last = order[2]
            here = axis_place(last)
            if k == 0:
                for j in range(1, 4):
                    self.go(0, self.share.at[pl.ds(lo, size)], self.spot(lo, size, ""), axis_peer(order[0], j))
            elif k == 1:
                spot = self.spot(lo, size, order[0])
                for j in range(1, 4):
                    self.go(1, spot, spot, axis_peer(order[1], j))
            elif k == 2:
                spot = self.spot(lo, size, order[:2])
                self.go(2, spot, spot, axis_peer(last, 1))
                self.go(2, spot, spot, axis_peer(last, 3))
                self.pass_on(spot)
            elif k == 3:
                before, after = lax.rem(here + 3, 4), lax.rem(here + 1, 4)
                cut = "x" if last == "z" else "z"
                low = self.spot(lo, size, order[:2], **{last: before, cut: pl.ds(0, 2)})
                high = self.spot(lo, size, order[:2], **{last: after, cut: pl.ds(2, 2)})
                self.go(3, low, low, axis_peer(last, 1))
                self.go(3, high, high, axis_peer(last, 3))
                self.pass_on(self.spot(lo, size, order[:2], **{last: before}))
                self.pass_on(self.spot(lo, size, order[:2], **{last: after}))
            elif k == 4:
                self.pass_on(self.spot(lo, size, order[:2], **{last: lax.rem(here + 2, 4)}))
        three = pl.ds(0, 3)
        if k == 0:
            self.kept = pltpu.make_async_copy(self.share, self.spot(0, self.share.shape[0], ""), self.own)
            self.kept.start()
            self.expect(0, ag.at[0, 0, 0, three])
        elif k == 1:
            self.expect(1, ag.at[0, 0, three])
        elif k == 2:
            self.expect(2, ag.at[0, pl.ds(0, 2)])
        elif k == 3:
            self.expect(3, ag.at[0, 0])
        elif k == 4:
            self.expect(4, ag.at[0])
        else:
            self.done()


class RowSwap(Steps):
    def __init__(self, src, dst, send, recv):
        super().__init__(send, recv)
        self.src, self.dst = src, dst

    def run(self, k):
        r, s = lax.axis_index("rows"), lax.axis_index("seq")
        if k == 0:
            for d in range(1, 8):
                peer = lax.rem(r + d, 8)
                self.go(0, self.src.at[peer], self.dst.at[r], (peer, s))
            self.dst[r] = self.src[r]
            self.expect(0, self.dst.at[pl.ds(0, 7)])
        else:
            self.done()


class RowGather(Steps):
    def __init__(self, dst, send, recv):
        super().__init__(send, recv)
        self.dst = dst

    def run(self, k):
        r = lax.axis_index("rows")
        dst = self.dst
        half = dst.shape[1] // 2
        before, after = lax.rem(r + 6, 8), lax.rem(r + 2, 8)
        if k == 0:
            for device in (axis_peer("y", 1), axis_peer("y", 3)):
                self.go(0, dst.at[r], dst.at[r], device)
            self.go(2, dst.at[r], dst.at[r], sibling())
            self.expect(0, dst.at[pl.ds(0, 2)])
        elif k == 1:
            low, high = dst.at[before, pl.ds(0, half)], dst.at[after, pl.ds(half, half)]
            self.go(1, low, low, axis_peer("y", 1))
            self.go(1, high, high, axis_peer("y", 3))
            for spot in (dst.at[before], dst.at[after]):
                self.go(2, spot, spot, sibling())
            self.expect(1, dst.at[0])
        elif k == 2:
            spot = dst.at[lax.rem(r + 4, 8)]
            self.go(2, spot, spot, sibling())
            self.expect(2, dst.at[pl.ds(0, 4)])
        else:
            self.done()


class Exchange:
    def __init__(self, src, dst, send, recv):
        self.src, self.dst, self.send, self.recv = src, dst, send, recv

    def all(self):
        r = lax.axis_index("rows")
        s = lax.axis_index("seq")
        for d in range(1, 16):
            peer = seq_peer(d)
            remote(self.src.at[peer], self.dst.at[s], self.send, self.recv, (r, peer)).start()
        self.dst[s] = self.src[s]
        return self

    def one(self, block):
        r = lax.axis_index("rows")
        s = lax.axis_index("seq")

        @pl.when(s != block)
        def _():
            remote(self.src.at[block], self.dst.at[s], self.send, self.recv, (r, block)).start()

        @pl.when(s == block)
        def _():
            self.dst[s] = self.src[block]

    def wait(self):
        gauge = self.dst.at[pl.ds(0, 15)]
        arrived(gauge, self.recv)
        arrived(gauge, self.send)


class Gather(Steps):
    def __init__(self, hall, send, recv):
        super().__init__(send, recv)
        self.hall = hall

    def run(self, k):
        z, x = axis_place("z"), axis_place("x")
        hall = self.hall
        if k == 0:
            for j in range(1, 4):
                self.go(0, hall.at[0, z, x], hall.at[0, z, x], axis_peer("x", j))
                self.go(0, hall.at[1, z, x], hall.at[1, z, x], axis_peer("z", j))
            self.expect(0, hall.at[:, pl.ds(0, 3), 0])
        elif k == 1:
            for j in (1, 3):
                self.go(1, hall.at[0, z], hall.at[0, z], axis_peer("z", j))
                self.go(1, hall.at[1, :, x], hall.at[1, :, x], axis_peer("x", j))
            self.expect(1, hall.at[0])
        elif k == 2:
            two, low = pl.ds(2, 2), pl.ds(0, 2)
            for spot, axis, j in (
                (hall.at[0, lax.rem(z + 3, 4), low], "z", 1),
                (hall.at[0, lax.rem(z + 1, 4), two], "z", 3),
                (hall.at[1, low, lax.rem(x + 3, 4)], "x", 1),
                (hall.at[1, two, lax.rem(x + 1, 4)], "x", 3),
            ):
                self.go(2, spot, spot, axis_peer(axis, j))
            self.expect(2, hall.at[:, :, 0])
        else:
            self.done()


class Heads(Steps):
    def __init__(self, part, sib_recv, both, y_recv, share, send, recv):
        super().__init__(send, recv)
        self.part, self.sib_recv, self.both, self.y_recv, self.share = part, sib_recv, both, y_recv, share

    def run(self, k):
        y = axis_place("y")
        if k == 0:
            self.go(0, self.part.at[1], self.sib_recv, sibling())
            self.expect(0, self.sib_recv)
        elif k == 1:
            self.both[...] = (self.part[0].astype(f32) + self.sib_recv[...].astype(f32)).astype(bf16)
            for j in range(1, 4):
                there = lax.rem(y + j, 4)
                self.go(1, self.both.at[pl.ds(there * SHARE, SHARE)], self.y_recv.at[j - 1], axis_peer("y", j))
            self.expect(1, self.y_recv)
        else:
            acc = self.both[pl.ds(y * SHARE, SHARE)].astype(f32)
            for j in range(3):
                acc = acc + self.y_recv[j].astype(f32)
            self.share[0:SHARE, :] = acc.astype(bf16)
            self.done()


class Quarters(Steps):
    def __init__(self, part, y_recv, send, recv):
        super().__init__(send, recv)
        self.part, self.y_recv = part, y_recv

    def run(self, k):
        y = axis_place("y")
        if k == 0:
            for j in range(1, 4):
                self.go(0, self.part.at[lax.rem(y + j, 4)], self.y_recv.at[j - 1], axis_peer("y", j))
            self.expect(0, self.y_recv)
        else:
            acc = self.part[y].astype(f32)
            for j in range(3):
                acc = acc + self.y_recv[j].astype(f32)
            self.done()
            return acc.astype(bf16)

    def total(self):
        self.collect()
        return self.run(1)


class Vectors:
    def __init__(self, buf, slots, send_sem, recv_sem):
        self.buf, self.slots, self.send_sem, self.recv_sem = buf, slots, send_sem, recv_sem
        self.at = 0

    def step(self):
        k = self.at
        self.at = k + 1
        if k == 0:
            value = self.buf[0]
        else:
            gauge = self.slots.at[k - 1, pl.ds(0, 3 if k < 4 else 1)]
            arrived(gauge, self.recv_sem.at[k - 1])
            arrived(gauge, self.send_sem.at[k - 1])
            value = self.slots[k - 1, 0]
            for j in range(1, 4 if k < 4 else 2):
                value = value + self.slots[k - 1, j]
        if k == 4:
            self.buf[1] = value
            return
        here = axis_place("xyz"[k]) if k < 3 else lax.rem(lax.axis_index("rows"), 2)
        devices = [axis_peer("xyz"[k], j) for j in range(1, 4)] if k < 3 else [sibling()]
        self.slots[k, here] = value
        for device in devices:
            spot = self.slots.at[k, here]
            remote(spot, spot, self.send_sem.at[k], self.recv_sem.at[k], device).start()


def block_kernel(
    offs_h, x_h, dy_h, ln1g_h, ln1b_h, bq_h, bv_h, bout_h, ln2g_h, ln2b_h, bup_h, bdown_h,
    wqkv_h, wout_h, wup_h, wdown_h,
    out_h, ig_h, ag0, ag1, agh, vecs_h,
    offs, x_ref, dy_ref, ln1g, ln1b, bq, bv, bout, ln2g, ln2b, bup, bdown,
    out_ref, ig_ref, vecs,
    wqkv, wout, wup, wdown, wsem,
    qkt, vals, rqk, rv, kn, vt, ot, lse, atts, ratt,
    hall, n1, rs1, h2ta, dya, actt, acta, gp, gpa, gb, gbs, attts, gres,
    gattt, rda, kt, vn, qn, don, dk, dv, dqkv, rdq,
    asend, arecv, ssend, srecv,
    *rest,
):
    (vbuf, vrecv, vsend, vrsem, lbuf, lrecv, lsend, lrsem, osem,
     hsend, hrecv, hpart, hsib, hboth, hy, hmine, wop, wor) = rest[:18]
    rest = rest[18:]
    sems = [rest[2 * k : 2 * k + 2] for k in range(12)]
    own, rest = rest[24], rest[25:]
    down_parts, down_recv1, down_mid, down_recv2 = [rest[2 * k : 2 * k + 2] for k in range(4)]
    up_parts, up_recv1, up_mid, up_recv2 = [rest[8 + 2 * k : 10 + 2 * k] for k in range(4)]
    out_parts, out_recv1, out_mid, out_recv2 = [rest[16 + 2 * k : 18 + 2 * k] for k in range(4)]
    down_share, up_share = rest[24:]
    loads = {}

    def load(name, src, dst):
        copy = pltpu.make_async_copy(src, dst, wsem.at[len(loads)])
        copy.start()
        loads[name] = copy

    load("x", x_h, x_ref)
    load("ln1g", ln1g_h, ln1g)
    load("ln1b", ln1b_h, ln1b)
    for t in (1, 0, 2):
        cols = pl.ds(t * D, D)
        load(f"qkv{t}", wqkv_h.at[:, cols], wqkv.at[:, cols])
    load("bq", bq_h, bq)
    load("bv", bv_h, bv)
    load("dy", dy_h, dy_ref)
    load("offs", offs_h, offs)
    load("out", wout_h, wout)
    for name, src, dst in (
        ("bout", bout_h, bout), ("ln2g", ln2g_h, ln2g), ("ln2b", ln2b_h, ln2b),
        ("bup", bup_h, bup), ("bdown", bdown_h, bdown),
    ):
        load(name, src, dst)
    load("up", wup_h, wup)
    load("down", wdown_h, wdown)
    stores = []

    def ready(*names):
        for name in names:
            loads[name].wait()

    def store(src, dst):
        copy = pltpu.make_async_copy(src, dst, osem.at[len(stores)])
        copy.start()
        stores.append(copy)

    bar, count = greet()
    vecg = vbuf.at[0]
    vecl = lbuf.at[0]
    early = Vectors(vbuf, vrecv, vsend, vrsem)
    late = Vectors(lbuf, lrecv, lsend, lrsem)
    gather = Gather(hall, hsend, hrecv)
    heads = Heads(hpart, hsib, hboth, hy, hmine, *sems[0])
    dy_rows = RowGather(dya, *sems[1])
    h2_rows = RowGather(h2ta, *sems[2])
    act_rows = RowSwap(actt, acta, *sems[3])
    gp_rows = RowSwap(gp, gpa, *sems[4])
    quarters = Quarters(wop, wor, *sems[5])
    down_sum = Scatter(CUT_DOWN, down_parts, down_recv1, down_mid, down_recv2, down_share, *sems[6])
    up_sum = Scatter(CUT_UP, up_parts, up_recv1, up_mid, up_recv2, up_share, *sems[7])
    down_all = Spread(down_share, ag0, WAYS_DOWN, *sems[8], own.at[0])
    up_all = Spread(up_share, ag1, WAYS_UP, *sems[9], own.at[1])
    head_all = Spread(hmine, agh, WAYS_LAST, *sems[10], own.at[2])
    out_sum = Scatter(CUT_OUT, out_parts, out_recv1, out_mid, out_recv2, hmine.at[pl.ds(SHARE, sum(CUT_OUT))], *sems[11])
    row = lax.axis_index("rows")

    def line(ref):
        return ref[...].astype(f32).reshape(1, D)

    core = lax.rem(lax.axis_index("rows"), 2)
    other = 1 - core
    sib = sibling()
    to_sib = []

    def send_sib(n, src, dst):
        copy = remote(src, dst, ssend.at[n], srecv.at[n], sib)
        copy.start()
        to_sib.append(copy)

    ready("x", "ln1g", "ln1b")
    x = x_ref[...].astype(f32)
    n, rs = norm_parts(x)
    n1[...] = n
    rs1[...] = rs
    h1f = n * line(ln1g) + line(ln1b)
    h1 = h1f.astype(bf16)
    for half in range(2):
        hall[half, axis_place("z"), axis_place("x")] = h1[:, half * 384 : (half + 1) * 384]
    for t in (1, 0, 2):
        ready(f"qkv{t}")
        y = dot(h1, wqkv[:, t * D : (t + 1) * D])
        if t == 0:
            ready("bq")
            y = y + line(bq)
        if t == 2:
            ready("bv")
            y = y + line(bv)
        low = jnp.transpose(y).astype(bf16).reshape(H, HS, TOK)
        if t < 2:
            qkt[:, t * HS : (t + 1) * HS, :] = low
        else:
            vals[...] = low
        if t == 0:
            pl.semaphore_wait(bar, count)
            moved = [Exchange(qkt, rqk, asend.at[0], arecv.at[0]).all()]
    moved.append(Exchange(vals, rv, asend.at[1], arecv.at[1]).all())
    ready("dy", "offs")
    dya[row] = dy_ref[...]
    dy_rows.step()
    for copy in moved:
        copy.wait()
    gather.step()

    attended = Exchange(atts, ratt, asend.at[2], arecv.at[2])
    attend_forward(
        offs, rqk, rv, kn, vt, ot, lse, atts,
        attended.one,
    )
    ready("out", "bout", "ln2g", "ln2b", "bup", "bdown", "up", "down")
    gather.step()
    attended.wait()
    dy_rows.step()

    att = jnp.transpose(ratt[...].reshape(D, TOK).astype(f32)).astype(bf16)
    send_sib(0, ratt.at[pl.ds(other * 8, 8)], attts)
    resid = x_ref[...].astype(f32) + dot(att, wout[...]) + line(bout)
    n2, rs2 = norm_parts(resid)
    h2f = n2 * line(ln2g) + line(ln2b)
    h2 = h2f.astype(bf16)
    h2ta[row] = jnp.transpose(h2f).astype(bf16)
    h2_rows.step()
    dy = dy_ref[...]
    down = None
    dh2 = None
    for c in range(4):
        cols = slice(c * D, (c + 1) * D)
        pre = dot(h2, wup[:, cols]) + bup[cols].astype(f32).reshape(1, D)
        square = pre * pre
        t = jnp.tanh(GELU_C * (pre + GELU_A * (square * pre)))
        act = 0.5 * pre * (1.0 + t)
        slope = 0.5 * (1.0 + t) + (0.5 * GELU_C) * pre * (1.0 - t * t) * (1.0 + (3.0 * GELU_A) * square)
        part = dot(act.astype(bf16), wdown[cols, :])
        down = part if down is None else down + part
        act_t = jnp.transpose(act).astype(bf16)
        actt[2 * c] = act_t[0:384]
        actt[2 * c + 1] = act_t[384:768]
        gpre = (dot_nt(dy, wdown[cols, :]) * slope).astype(bf16)
        gp[2 * c] = gpre[:, 0:384]
        gp[2 * c + 1] = gpre[:, 384:768]
        vecg[BUP + c : BUP + c + 1, :] = over_tokens(gpre.astype(f32))
        part = dot_nt(gpre, wup[:, cols])
        dh2 = part if dh2 is None else dh2 + part
    act_rows.step()
    gp_rows.step()
    out_ref[...] = (resid + down + line(bdown)).astype(bf16)
    store(out_ref, out_h)
    vecg[BDOWN : BDOWN + 1, :] = over_tokens(dy.astype(f32))
    vecg[LN2G : LN2G + 1, :] = over_tokens(dh2 * n2)
    vecg[LN2B : LN2B + 1, :] = over_tokens(dh2)
    grad = dy.astype(f32) + norm_back(dh2, n2, rs2, line(ln2g))
    gres[...] = grad
    branch = grad.astype(bf16)
    gb[...] = branch
    vecg[BOUT : BOUT + 1, :] = over_tokens(branch.astype(f32))
    gattt[...] = jnp.transpose(dot_nt(branch, wout[...])).astype(bf16).reshape(H, HS, TOK)
    moved = Exchange(gattt, rda, asend.at[3], arecv.at[3]).all()
    h2_rows.step()
    send_sib(1, gb, gbs)

    gather.step()
    moved.wait()

    def part_out():
        for copy in to_sib:
            copy.wait()
        left = jnp.concatenate(
            [ratt[pl.ds(core * 8, 8)].reshape(384, TOK), attts[...].reshape(384, TOK)], axis=1
        )
        right = jnp.concatenate([gb[...], gbs[...]], axis=0)
        res = dot(left, right).astype(bf16)
        for k in range(4):
            for t in range(6):
                wop[k, t * 96 : (t + 1) * 96, :] = res[k * 96 : (k + 1) * 96, t * TOK : (t + 1) * TOK]
        quarters.step()

    def grads_down():
        dy_rows.step()
        act_rows.step()
        left = jnp.concatenate([acta[k] for k in range(8)], axis=1)
        res = dot(left, dya[...].reshape(8 * TOK, D)).astype(bf16)
        for t in range(6):
            down_sum.put(res[:, t * TOK : (t + 1) * TOK], t * 384)
        down_sum.step()

    def grads_up():
        h2_rows.step()
        gp_rows.step()
        left = jnp.concatenate([h2ta[k] for k in range(8)], axis=1)
        res = dot(left, gpa[...].reshape(8 * TOK, 384)).astype(bf16)
        for t in range(3):
            up_sum.put(res[:, t * TOK : (t + 1) * TOK], t * D)
        up_sum.step()

    def grads_out():
        out_sum.put(quarters.total(), 0)
        out_sum.put(jnp.zeros((192, TOK), bf16), 576)
        out_sum.step()

    back = Exchange(dqkv, rdq, asend.at[4], arecv.at[4])

    def between(i):
        for half in (0, 1):
            back.one(2 * i + half)
        if i == 7:
            dy_rows.step()
            early.step()
        elif i == 6:
            part_out()
        elif i == 4:
            grads_down()
        elif i == 1:
            down_sum.step()

    attend_backward(offs, rqk, rv, kn, kt, vn, qn, don, rda, ot, lse, dqkv, dk, dv, between)
    h2_rows.step()
    grads_up()
    back.wait()

    dh1t = None
    ones = jnp.ones((8, TOK), bf16)
    for t in range(3):
        grad_t = rdq[:, t * HS : (t + 1) * HS, :].reshape(D, TOK)
        part = dot(wqkv[:, t * D : (t + 1) * D], grad_t)
        dh1t = part if dh1t is None else dh1t + part
        if t != 1:
            row = BQ if t == 0 else BV
            vecl[row : row + 1, :] = dot_nt(ones, grad_t)[0:1, :]
    dh1 = jnp.transpose(dh1t)
    n = n1[...]
    vecl[LN1G : LN1G + 1, :] = over_tokens(dh1 * n)
    vecl[LN1B : LN1B + 1, :] = over_tokens(dh1)
    vecl[4:8, :] = jnp.zeros((4, D), f32)
    gather.step()
    spread = jnp.concatenate([dqkv[k] for k in range(NB)], axis=1)

    def part_head(slot, half):
        res = dot(spread, hall[half].reshape(SEQ, 384)).astype(bf16)
        for u in range(3):
            hpart[slot, u * 144 : (u + 1) * 144, :] = res[:, u * TOK : (u + 1) * TOK]
        hpart[slot, 432:HEAD_ROWS, :] = jnp.zeros((HEAD_ROWS - 432, TOK), bf16)

    part_head(1, other)
    heads.step()
    down_sum.step()
    down_all.step()
    part_head(0, core)
    early.step()
    late.step()
    grads_out()
    heads.step()
    up_sum.step()
    down_all.step()
    late.step()
    ig_ref[...] = (gres[...] + norm_back(dh1, n, rs1[...], line(ln1g))).astype(bf16)
    store(ig_ref, ig_h)
    out_sum.step()
    heads.step()
    early.step()
    up_sum.step()
    up_all.step()
    down_all.step()
    late.step()
    out_sum.step()
    head_all.step()
    up_all.step()
    early.step()
    down_all.step()
    late.step()
    head_all.step()
    late.step()
    early.step()
    vecs[0] = vbuf[1]
    vecs[1] = lbuf[1]
    store(vecs, vecs_h)
    up_all.step()
    head_all.step()
    up_all.step()
    head_all.step()
    down_all.step()
    up_all.step()
    head_all.step()
    for item in (down_all, up_all, head_all):
        item.step()
    for item in (down_sum, up_sum, out_sum):
        item.done()
    for copy in stores:
        copy.wait()


VMEM = pl.BlockSpec(memory_space=pltpu.VMEM)
SMEM = pl.BlockSpec(memory_space=pltpu.SMEM)
ANY = pl.BlockSpec(memory_space=pl.ANY)


def call_block(offsets, x, dy, vectors, weights):
    v = pltpu.VMEM
    dma = pltpu.SemaphoreType.DMA
    shape = jax.ShapeDtypeStruct
    return pl.pallas_call(
        block_kernel,
        out_shape=(
            shape((TOK, D), bf16),
            shape((TOK, D), bf16),
            shape((2, 4, 4, 4, sum(CUT_DOWN), TOK), bf16),
            shape((2, 4, 4, 4, sum(CUT_UP), TOK), bf16),
            shape((2, 4, 4, 4, ROWS_LAST, TOK), bf16),
            shape((2, VROWS, D), f32),
        ),
        in_specs=[ANY] * 16,
        out_specs=(ANY,) * 6,
        scratch_shapes=[
            pltpu.SMEM((1, 8), jnp.int32), v((TOK, D), bf16), v((TOK, D), bf16),
            *[v((FF if k == 7 else D,), bf16) for k in range(9)],
            v((TOK, D), bf16), v((TOK, D), bf16), v((2, VROWS, D), f32),
            v((D, 3 * D), bf16), v((D, D), bf16), v((D, FF), bf16), v((FF, D), bf16), dma((20,)),
            v((NB, 96, TOK), bf16), v((NB, HS, TOK), bf16), v((NB, 96, TOK), bf16), v((NB, HS, TOK), bf16),
            v((SEQ, HS), bf16), v((HS, SEQ), bf16),
            v((HS, SEQ), f32), v((1, SEQ), f32), v((NB, HS, TOK), bf16), v((NB, HS, TOK), bf16),
            v((2, 4, 4, TOK, 384), bf16), v((TOK, D), f32), v((TOK, 1), f32),
            v((8, D, TOK), bf16), v((8, TOK, D), bf16),
            v((8, 384, TOK), bf16), v((8, 384, TOK), bf16), v((8, TOK, 384), bf16), v((8, TOK, 384), bf16),
            v((TOK, D), bf16), v((TOK, D), bf16), v((8, HS, TOK), bf16), v((TOK, D), f32),
            v((NB, HS, TOK), bf16), v((NB, HS, TOK), bf16),
            v((HS, SEQ), bf16), v((SEQ, HS), bf16), v((SEQ, HS), bf16), v((SEQ, HS), bf16),
            v((SEQ, HS), f32), v((SEQ, HS), f32),
            v((NB, 144, TOK), bf16), v((NB, 144, TOK), bf16),
            dma((5,)), dma((5,)), dma((2,)), dma((2,)),
            v((2, VROWS, D), f32), v((4, 4, VROWS, D), f32), dma((4,)), dma((4,)),
            v((2, VROWS, D), f32), v((4, 4, VROWS, D), f32), dma((4,)), dma((4,)), dma((3,)),
            dma((3,)), dma((3,)), v((2, HEAD_ROWS, TOK), bf16), v((HEAD_ROWS, TOK), bf16),
            v((HEAD_ROWS, TOK), bf16), v((3, SHARE, TOK), bf16), v((ROWS_LAST, TOK), bf16),
            v((4, 576, TOK), bf16), v((3, 576, TOK), bf16),
            *[dma((n,)) for n in (2, 3, 3, 1, 1, 1, 4, 4, 5, 5, 5, 4) for _ in range(2)], dma((3,)),
            *[
                v(lead + (cut, TOK), bf16)
                for cuts in (CUT_DOWN, CUT_UP, CUT_OUT)
                for lead in ((4, 4), (3, 4), (4,), (3,))
                for cut in cuts
            ],
            v((sum(CUT_DOWN), TOK), bf16), v((sum(CUT_UP), TOK), bf16),
        ],
        compiler_params=pltpu.CompilerParams(
            collective_id=1, has_side_effects=True, vmem_limit_bytes=58 * 2**20
        ),
    )(offsets, x, dy, *vectors, *weights)


def widen_kernel(ag0, ag1, agh, vecs_h, done_h, ig_h, wqkv, wout, wup, wdown, out_h, grad_h, *rest):
    small_h, small = rest[:9], rest[9:18]
    vecs, vsem, ssem, down_in, up_in, out_in, down_out, up_out, out_out, headb, wideb, isem, osem = (
        rest[18], rest[19], rest[20], rest[21:23], rest[23:25], rest[25:27], *rest[27:]
    )
    passed = [
        pltpu.make_async_copy(done_h, out_h, vsem.at[0]),
        pltpu.make_async_copy(ig_h, grad_h, vsem.at[1]),
    ]
    fetch = pltpu.make_async_copy(vecs_h, vecs, vsem.at[2])

    def share_loads(kind, k):
        ag, cuts, bufs, lo = ((ag0, CUT_DOWN, down_in, 0), (ag1, CUT_UP, up_in, 0), (agh, CUT_OUT, out_in, SHARE))[kind]
        copies = []
        for n in range(2):
            src = ag.at[k % 2, :, :, k // 2, pl.ds(lo, cuts[n])]
            copies.append(pltpu.make_async_copy(src, bufs[n].at[k], isem.at[kind, k, n]))
            lo += cuts[n]
        return copies

    def pieces(cuts, offset, rows):
        at = 0
        while at < rows:
            n = 0 if offset < 16 * cuts[0] else 1
            inside = offset - n * 16 * cuts[0]
            block, lo = inside // cuts[n], inside % cuts[n]
            size = min(cuts[n] - lo, rows - at)
            yield at, size, n, block, lo
            at += size
            offset += size

    def widen(bufs, cuts, k, offset, rows, dst, col):
        for at, size, n, block, lo in pieces(cuts, offset, rows):
            part = bufs[n][k, block // 4, block % 4, lo : lo + size, :]
            dst[at : at + size, col * TOK : (col + 1) * TOK] = part.astype(f32)

    down_store = [
        pltpu.make_async_copy(down_out.at[k % 3], wdown.at[pl.ds(k * 384, 384)], osem.at[0, k % 3]) for k in range(8)
    ]
    up_store = [
        pltpu.make_async_copy(up_out.at[k % 3], wup.at[:, pl.ds(k * 384, 384)], osem.at[1, k % 3]) for k in range(8)
    ]
    out_store = [
        pltpu.make_async_copy(
            out_out.at[k % 3], wout.at[pl.ds((k % 2) * 384 + (k // 2) * 96, 96)], osem.at[2, k % 3]
        )
        for k in range(8)
    ]

    cuts_head = (((0, 0, 112, 0), (1, 0, 32, 112)), ((1, 32, 80, 0), (2, 0, 64, 80)), ((2, 64, 48, 0), (3, 0, 96, 48)))

    def head_loads(k):
        return [
            pltpu.make_async_copy(
                agh.at[k // 3, :, :, y, pl.ds(lo, size)], headb.at[k, :, :, pl.ds(to, size)], isem.at[3, k, n]
            )
            for n, (y, lo, size, to) in enumerate(cuts_head[k % 3])
        ]

    head_store = [
        pltpu.make_async_copy(wideb.at[k % 3], wqkv.at[pl.ds(k * TOK, TOK)], osem.at[3, k % 3]) for k in range(6)
    ]

    fetch.start()
    for k in range(8):
        for copy in share_loads(0, k) + share_loads(1, k) + share_loads(2, k) + (head_loads(k) if k < 6 else []):
            copy.start()
    for copy in passed:
        copy.start()
    for k in range(8):
        for copy in share_loads(0, k):
            copy.wait()
        if k >= 3:
            down_store[k - 3].wait()
        for t in range(6):
            widen(down_in, CUT_DOWN, k, t * 384, 384, down_out.at[k % 3], t)
        down_store[k].start()
        for copy in share_loads(1, k):
            copy.wait()
        if k >= 3:
            up_store[k - 3].wait()
            out_store[k - 3].wait()
        for t in range(3):
            widen(up_in, CUT_UP, k, t * D, D, up_out.at[k % 3], t)
        up_store[k].start()
        for copy in share_loads(2, k):
            copy.wait()
        for t in range(6):
            widen(out_in, CUT_OUT, k, t * 96, 96, out_out.at[k % 3], t)
        out_store[k].start()
        if k < 6:
            for copy in head_loads(k):
                copy.wait()
            if k >= 3:
                head_store[k - 3].wait()
            for t in range(3):
                block = headb[k, :, :, t * HS : (t + 1) * HS, :].reshape(D, TOK)
                wideb[k % 3, :, t * D : (t + 1) * D] = jnp.transpose(block.astype(f32))
            head_store[k].start()
        if k == 0:
            fetch.wait()
            places = ((1, LN1G), (1, LN1B), (1, BQ), (1, BV), (0, BOUT), (0, LN2G), (0, LN2B), (0, BUP), (0, BDOWN))
            for n, (ref, (group, line)) in enumerate(zip(small, places)):
                if line == BUP:
                    for c in range(4):
                        ref[c * D : (c + 1) * D] = vecs[0, BUP + c : BUP + c + 1, :].reshape(D)
                else:
                    ref[...] = vecs[group, line : line + 1, :].reshape(D)
                copy = pltpu.make_async_copy(ref, small_h[n], ssem.at[n])
                copy.start()
                passed.append(copy)
    for k in range(5, 8):
        down_store[k].wait()
        up_store[k].wait()
        out_store[k].wait()
        head_store[k - 2].wait()
    for copy in passed:
        copy.wait()


def call_widen(*arrays):
    v = pltpu.VMEM
    dma = pltpu.SemaphoreType.DMA
    shape = jax.ShapeDtypeStruct
    return pl.pallas_call(
        widen_kernel,
        out_shape=(
            shape((D, 3 * D), f32), shape((D, D), f32), shape((D, FF), f32), shape((FF, D), f32),
            shape((TOK, D), bf16), shape((TOK, D), bf16),
        ) + tuple(shape((FF if k == 7 else D,), f32) for k in range(9)),
        in_specs=[ANY] * 6,
        out_specs=(ANY,) * 15,
        scratch_shapes=[
            *[v((FF if k == 7 else D,), f32) for k in range(9)], v((2, VROWS, D), f32), dma((3,)), dma((9,)),
            *[v((8, 4, 4, cut, TOK), bf16) for cut in CUT_DOWN + CUT_UP + CUT_OUT],
            v((3, 384, D), f32), v((3, D, 384), f32), v((3, 96, D), f32),
            v((6, 4, 4, 144, TOK), bf16), v((3, TOK, 3 * D), f32), dma((4, 8, 2)), dma((4, 3)),
        ],
        compiler_params=pltpu.CompilerParams(vmem_limit_bytes=58 * 2**20),
    )(*arrays)


def local(
    block_input, offsets, ln1_gain, ln1_bias, w_qkv, bias_query, bias_value, w_out, bias_out,
    ln2_gain, ln2_bias, w_up, bias_up, w_down, bias_down, cotangent,
):
    out, ig, ag0, ag1, agh, vecs = call_block(
        offsets, block_input.reshape(TOK, D), cotangent.reshape(TOK, D),
        (ln1_gain, ln1_bias, bias_query, bias_value, bias_out, ln2_gain, ln2_bias, bias_up, bias_down),
        (w_qkv, w_out, w_up, w_down),
    )
    wide = call_widen(ag0, ag1, agh, vecs, out, ig)
    g_qkv, g_out, g_up, g_down, out, ig = wide[:6]
    s = wide[6:]
    return (
        out.reshape(1, TOK, D), ig.reshape(1, TOK, D),
        s[0], s[1], g_qkv, s[2], s[3], g_out, s[4], s[5], s[6], g_up, s[7], g_down, s[8],
    )


def solution(mesh):
    tokens = P("rows", "seq", None)
    return jax.shard_map(
        local,
        mesh=mesh,
        in_specs=(tokens, P("rows", None)) + (P(),) * 13 + (tokens,),
        out_specs=(tokens, tokens) + (P(),) * 13,
        check_vma=False,
    )
```

time: 134 us -> 128 us (0.955)
  Pallas kernels: 132 us -> 126 us
    pallas_call x1, Pallas kernels: 117 us -> 111 us  [call_block(): pl.pallas_call(block_kernel, out_shape=(shape((TOK, D), bf16), shape((TOK...]
where the time goes in v3:
time: 128 us; the launch traced here: 127 us
  Pallas kernels  126 us (98%)
    pallas_call x1, Pallas kernels, call_block(): pl.pallas_call(block_kernel, out_shape=(shape((TOK, D), bf16), shape((TOK...  111 us
    pallas_call x1, Pallas kernels, call_widen(): pl.pallas_call(widen_kernel, out_shape=(shape((D, 3 * D), f32), shape((D,...  15.5 us

profile of v3, /device:TPU:1, one launch (start us, length us, event | category | flops | bytes accessed | tf_op | source)
XLA Modules:
  0.0 127.3 jit_solution(3638837765972595030)
XLA Ops:
  0.7 111.0 %shard_map.271 = (bf16[128,768]{1,0:T(8,128)(2,1)}, bf16[128,768]{1,0:T(8,128)(2,1)}, bf16[2,4,4,4,144,128]{5,4,3,2,1,0:T(8,128)(2,1)}, bf16[2,4,4,4,144,128]{5,...) custom-call(s32[1,8]{1,0:T(1,128)} %offs_h.1, bf16[128,768]{1,0:T(8,128)(2,1)} %bitcast.4, ...), custom_call_target="tpu_custom_call" | custom-call | tf_op jit(solution)/shard_map/pallas_call | solution.py:867
  111.7 15.5 %shard_map.272 = (f32[768,2304]{1,0:T(8,128)}, f32[768,768]{1,0:T(8,128)}, f32[768,3072]{1,0:T(8,128)}, f32[3072,768]{1,0:T(8,128)}, bf16[128,768]{1,0:T(8,128)(...) custom-call(bf16[2,4,4,4,144,128]{5,4,3,2,1,0:T(8,128)(2,1)} %get-tu, ...), custom_call_target="tpu_custom_call" | custom-call | tf_op jit(solution)/shard_map/pallas_call | solution.py:1040

commit v4 on v3

--- a/solution.py
+++ b/solution.py
@@ -858,6 +858,7 @@
 VMEM = pl.BlockSpec(memory_space=pltpu.VMEM)
 SMEM = pl.BlockSpec(memory_space=pltpu.SMEM)
 ANY = pl.BlockSpec(memory_space=pl.ANY)
+HBM = pl.BlockSpec(memory_space=pltpu.HBM)
 
 
 def call_block(offsets, x, dy, vectors, weights):
@@ -867,14 +868,14 @@
     return pl.pallas_call(
         block_kernel,
         out_shape=(
-            shape((TOK, D), bf16),
-            shape((TOK, D), bf16),
-            shape((2, 4, 4, 4, sum(CUT_DOWN), TOK), bf16),
-            shape((2, 4, 4, 4, sum(CUT_UP), TOK), bf16),
-            shape((2, 4, 4, 4, ROWS_LAST, TOK), bf16),
-            shape((2, VROWS, D), f32),
+            v((TOK, D), bf16),
+            v((TOK, D), bf16),
+            v((2, 4, 4, 4, sum(CUT_DOWN), TOK), bf16),
+            v((2, 4, 4, 4, sum(CUT_UP), TOK), bf16),
+            v((2, 4, 4, 4, ROWS_LAST, TOK), bf16),
+            v((2, VROWS, D), f32),
         ),
-        in_specs=[ANY] * 16,
+        in_specs=[HBM] * 16,
         out_specs=(ANY,) * 6,
         scratch_shapes=[
             pltpu.SMEM((1, 8), jnp.int32), v((TOK, D), bf16), v((TOK, D), bf16),
@@ -908,46 +909,44 @@
             v((sum(CUT_DOWN), TOK), bf16), v((sum(CUT_UP), TOK), bf16),
         ],
         compiler_params=pltpu.CompilerParams(
-            collective_id=1, has_side_effects=True, vmem_limit_bytes=58 * 2**20
+            collective_id=1, has_side_effects=True, vmem_limit_bytes=43 * 2**20
         ),
-    )(offsets, x, dy, *vectors, *weights)
-
-
-def widen_kernel(ag0, ag1, agh, vecs_h, done_h, ig_h, wqkv, wout, wup, wdown, out_h, grad_h, *rest):
+    )(*[pltpu.with_memory_space_constraint(a, pltpu.HBM) for a in (offsets, x, dy, *vectors, *weights)])
+
+
+def widen_kernel(ag0, ag1, agh, vecs, done_h, ig_h, wqkv, wout, wup, wdown, out_h, grad_h, *rest):
     small_h, small = rest[:9], rest[9:18]
-    vecs, vsem, ssem, down_in, up_in, out_in, down_out, up_out, out_out, headb, wideb, isem, osem = (
-        rest[18], rest[19], rest[20], rest[21:23], rest[23:25], rest[25:27], *rest[27:]
-    )
+    down_out, up_out, out_out, wideb, vsem, ssem, osem = rest[18:]
     passed = [
         pltpu.make_async_copy(done_h, out_h, vsem.at[0]),
         pltpu.make_async_copy(ig_h, grad_h, vsem.at[1]),
     ]
-    fetch = pltpu.make_async_copy(vecs_h, vecs, vsem.at[2])
-
-    def share_loads(kind, k):
-        ag, cuts, bufs, lo = ((ag0, CUT_DOWN, down_in, 0), (ag1, CUT_UP, up_in, 0), (agh, CUT_OUT, out_in, SHARE))[kind]
-        copies = []
-        for n in range(2):
-            src = ag.at[k % 2, :, :, k // 2, pl.ds(lo, cuts[n])]
-            copies.append(pltpu.make_async_copy(src, bufs[n].at[k], isem.at[kind, k, n]))
-            lo += cuts[n]
-        return copies
-
-    def pieces(cuts, offset, rows):
+
+    def pieces(cuts, base, offset, rows):
         at = 0
         while at < rows:
             n = 0 if offset < 16 * cuts[0] else 1
             inside = offset - n * 16 * cuts[0]
             block, lo = inside // cuts[n], inside % cuts[n]
             size = min(cuts[n] - lo, rows - at)
-            yield at, size, n, block, lo
+            yield at, size, block // 4, block % 4, base + n * cuts[0] + lo
             at += size
             offset += size
 
-    def widen(bufs, cuts, k, offset, rows, dst, col):
-        for at, size, n, block, lo in pieces(cuts, offset, rows):
-            part = bufs[n][k, block // 4, block % 4, lo : lo + size, :]
+    def widen(ag, cuts, base, k, offset, rows, dst, col):
+        for at, size, z, x, lo in pieces(cuts, base, offset, rows):
+            part = ag[k % 2, z, x, k // 2, lo : lo + size, :]
             dst[at : at + size, col * TOK : (col + 1) * TOK] = part.astype(f32)
+
+    def head_rows(core, z, x, lo, rows):
+        parts = []
+        while rows:
+            y, inside = lo // SHARE, lo % SHARE
+            size = min(SHARE - inside, rows)
+            parts.append(agh[core, z, x, y, inside : inside + size, :])
+            lo += size
+            rows -= size
+        return parts
 
     down_store = [
         pltpu.make_async_copy(down_out.at[k % 3], wdown.at[pl.ds(k * 384, 384)], osem.at[0, k % 3]) for k in range(8)
@@ -961,59 +960,37 @@
         )
         for k in range(8)
     ]
-
-    cuts_head = (((0, 0, 112, 0), (1, 0, 32, 112)), ((1, 32, 80, 0), (2, 0, 64, 80)), ((2, 64, 48, 0), (3, 0, 96, 48)))
-
-    def head_loads(k):
-        return [
-            pltpu.make_async_copy(
-                agh.at[k // 3, :, :, y, pl.ds(lo, size)], headb.at[k, :, :, pl.ds(to, size)], isem.at[3, k, n]
-            )
-            for n, (y, lo, size, to) in enumerate(cuts_head[k % 3])
-        ]
-
     head_store = [
         pltpu.make_async_copy(wideb.at[k % 3], wqkv.at[pl.ds(k * TOK, TOK)], osem.at[3, k % 3]) for k in range(6)
     ]
-
-    fetch.start()
-    for k in range(8):
-        for copy in share_loads(0, k) + share_loads(1, k) + share_loads(2, k) + (head_loads(k) if k < 6 else []):
-            copy.start()
     for copy in passed:
         copy.start()
     for k in range(8):
-        for copy in share_loads(0, k):
-            copy.wait()
         if k >= 3:
             down_store[k - 3].wait()
         for t in range(6):
-            widen(down_in, CUT_DOWN, k, t * 384, 384, down_out.at[k % 3], t)
+            widen(ag0, CUT_DOWN, 0, k, t * 384, 384, down_out.at[k % 3], t)
         down_store[k].start()
-        for copy in share_loads(1, k):
-            copy.wait()
         if k >= 3:
             up_store[k - 3].wait()
             out_store[k - 3].wait()
         for t in range(3):
-            widen(up_in, CUT_UP, k, t * D, D, up_out.at[k % 3], t)
+            widen(ag1, CUT_UP, 0, k, t * D, D, up_out.at[k % 3], t)
         up_store[k].start()
-        for copy in share_loads(2, k):
-            copy.wait()
         for t in range(6):
-            widen(out_in, CUT_OUT, k, t * 96, 96, out_out.at[k % 3], t)
+            widen(agh, CUT_OUT, SHARE, k, t * 96, 96, out_out.at[k % 3], t)
         out_store[k].start()
         if k < 6:
-            for copy in head_loads(k):
-                copy.wait()
             if k >= 3:
                 head_store[k - 3].wait()
             for t in range(3):
-                block = headb[k, :, :, t * HS : (t + 1) * HS, :].reshape(D, TOK)
+                parts = []
+                for head in range(H):
+                    parts += head_rows(k // 3, head // 4, head % 4, (k % 3) * 144 + t * HS, HS)
+                block = jnp.concatenate(parts, axis=0)
                 wideb[k % 3, :, t * D : (t + 1) * D] = jnp.transpose(block.astype(f32))
             head_store[k].start()
         if k == 0:
-            fetch.wait()
             places = ((1, LN1G), (1, LN1B), (1, BQ), (1, BV), (0, BOUT), (0, LN2G), (0, LN2B), (0, BUP), (0, BDOWN))
             for n, (ref, (group, line)) in enumerate(zip(small, places)):
                 if line == BUP:
@@ -1043,16 +1020,15 @@
             shape((D, 3 * D), f32), shape((D, D), f32), shape((D, FF), f32), shape((FF, D), f32),
             shape((TOK, D), bf16), shape((TOK, D), bf16),
         ) + tuple(shape((FF if k == 7 else D,), f32) for k in range(9)),
-        in_specs=[ANY] * 6,
+        in_specs=[VMEM] * 4 + [ANY] * 2,
         out_specs=(ANY,) * 15,
         scratch_shapes=[
-            *[v((FF if k == 7 else D,), f32) for k in range(9)], v((2, VROWS, D), f32), dma((3,)), dma((9,)),
-            *[v((8, 4, 4, cut, TOK), bf16) for cut in CUT_DOWN + CUT_UP + CUT_OUT],
-            v((3, 384, D), f32), v((3, D, 384), f32), v((3, 96, D), f32),
-            v((6, 4, 4, 144, TOK), bf16), v((3, TOK, 3 * D), f32), dma((4, 8, 2)), dma((4, 3)),
+            *[v((FF if k == 7 else D,), f32) for k in range(9)],
+            v((3, 384, D), f32), v((3, D, 384), f32), v((3, 96, D), f32), v((3, TOK, 3 * D), f32),
+            dma((2,)), dma((9,)), dma((4, 3)),
         ],
-        compiler_params=pltpu.CompilerParams(vmem_limit_bytes=58 * 2**20),
-    )(*arrays)
+        compiler_params=pltpu.CompilerParams(vmem_limit_bytes=30 * 2**20),
+    )(*[pltpu.with_memory_space_constraint(a, pltpu.VMEM) for a in arrays])
 
 
 def local(

time: 128 us -> 121 us (0.945)
  Pallas kernels: 126 us -> 121 us
    pallas_call x1, Pallas kernels: 15.5 us -> 9.93 us  [call_widen(): pl.pallas_call(widen_kernel, out_shape=(shape((D, 3 * D), f32), shape((D,...]
where the time goes in v4:
time: 121 us
  Pallas kernels  121 us (100%)
    pallas_call x1, Pallas kernels, call_block(): pl.pallas_call(block_kernel, out_shape=(v((TOK, D), bf16), v((TOK, D), bf...  111 us
    pallas_call x1, Pallas kernels, call_widen(): pl.pallas_call(widen_kernel, out_shape=(shape((D, 3 * D), f32), shape((D,...  9.93 us

profile of v4, /device:TPU:1, one launch (start us, length us, event | category | flops | bytes accessed | tf_op | source)
XLA Modules:
  0.0 121.4 jit_solution(11254597673212322239)
XLA Ops:
  0.7 110.6 %shard_map.271 = (bf16[128,768]{1,0:T(8,128)(2,1)S(1)}, bf16[128,768]{1,0:T(8,128)(2,1)S(1)}, bf16[2,4,4,4,144,128]{5,4,3,2,1,0:T(8,128)(2,1)S(1)}, bf16[2,4,4,4...) custom-call(s32[1,8]{1,0:T(1,128)} %offs_h.1, ...), custom_call_target="tpu_custom_call" | custom-call | tf_op jit(solution)/shard_map/pallas_call | solution.py:868
  111.2 9.9 %shard_map.272 = (f32[768,2304]{1,0:T(8,128)}, f32[768,768]{1,0:T(8,128)}, f32[768,3072]{1,0:T(8,128)}, f32[3072,768]{1,0:T(8,128)}, bf16[128,768]{1,0:T(8,128)(...) custom-call(bf16[2,4,4,4,144,128]{5,4,3,2,1,0:T(8,128)(2,1)S(1)} %ge, ...), custom_call_target="tpu_custom_call" | custom-call | tf_op jit(solution)/shard_map/pallas_call | solution.py:1017

commit v5 on v4

--- a/solution.py
+++ b/solution.py
@@ -24,10 +24,10 @@
 CUT_OUT = (32, 16)
 SHARE = 112
 HEAD_ROWS = 4 * SHARE
-ROWS_LAST = SHARE + sum(CUT_OUT)
 WAYS_DOWN = ((0, 48, "xzy"), (48, 48, "zyx"), (96, 48, "yxz"))
 WAYS_UP = WAYS_DOWN
-WAYS_LAST = ((0, 64, "xzy"), (64, 48, "zyx"), (112, 48, "yxz"))
+WAYS_HEAD = ((0, 48, "xzy"), (48, 32, "zyx"), (80, 32, "yxz"))
+WAYS_OUT = ((0, 16, "xzy"), (16, 16, "zyx"), (32, 16, "yxz"))
 SCALE = HS**-0.5
 SCALE_LOG2E = SCALE * 1.4426950408889634
 NEGATIVE = -1e30
@@ -547,11 +547,11 @@
 def block_kernel(
     offs_h, x_h, dy_h, ln1g_h, ln1b_h, bq_h, bv_h, bout_h, ln2g_h, ln2b_h, bup_h, bdown_h,
     wqkv_h, wout_h, wup_h, wdown_h,
-    out_h, ig_h, ag0, ag1, agh, vecs_h,
+    out_h, ig_h, ag0, ag1, agh, agw, vecs_h,
     offs, x_ref, dy_ref, ln1g, ln1b, bq, bv, bout, ln2g, ln2b, bup, bdown,
     out_ref, ig_ref, vecs,
     wqkv, wout, wup, wdown, wsem,
-    qkt, vals, rqk, rv, kn, vt, ot, lse, atts, ratt,
+    qkvt, rqk, kn, vt, ot, lse, atts, ratt,
     hall, n1, rs1, h2ta, dya, actt, acta, gp, gpa, gb, gbs, attts, gres,
     gattt, rda, kt, vn, qn, don, dk, dv, dqkv, rdq,
     asend, arecv, ssend, srecv,
@@ -560,12 +560,12 @@
     (vbuf, vrecv, vsend, vrsem, lbuf, lrecv, lsend, lrsem, osem,
      hsend, hrecv, hpart, hsib, hboth, hy, hmine, wop, wor) = rest[:18]
     rest = rest[18:]
-    sems = [rest[2 * k : 2 * k + 2] for k in range(12)]
-    own, rest = rest[24], rest[25:]
+    sems = [rest[2 * k : 2 * k + 2] for k in range(13)]
+    own, rest = rest[26], rest[27:]
     down_parts, down_recv1, down_mid, down_recv2 = [rest[2 * k : 2 * k + 2] for k in range(4)]
     up_parts, up_recv1, up_mid, up_recv2 = [rest[8 + 2 * k : 10 + 2 * k] for k in range(4)]
     out_parts, out_recv1, out_mid, out_recv2 = [rest[16 + 2 * k : 18 + 2 * k] for k in range(4)]
-    down_share, up_share = rest[24:]
+    down_share, up_share, out_share = rest[24:]
     loads = {}
 
     def load(name, src, dst):
@@ -583,14 +583,6 @@
     load("bv", bv_h, bv)
     load("dy", dy_h, dy_ref)
     load("offs", offs_h, offs)
-    load("out", wout_h, wout)
-    for name, src, dst in (
-        ("bout", bout_h, bout), ("ln2g", ln2g_h, ln2g), ("ln2b", ln2b_h, ln2b),
-        ("bup", bup_h, bup), ("bdown", bdown_h, bdown),
-    ):
-        load(name, src, dst)
-    load("up", wup_h, wup)
-    load("down", wdown_h, wdown)
     stores = []
 
     def ready(*names):
@@ -618,8 +610,9 @@
     up_sum = Scatter(CUT_UP, up_parts, up_recv1, up_mid, up_recv2, up_share, *sems[7])
     down_all = Spread(down_share, ag0, WAYS_DOWN, *sems[8], own.at[0])
     up_all = Spread(up_share, ag1, WAYS_UP, *sems[9], own.at[1])
-    head_all = Spread(hmine, agh, WAYS_LAST, *sems[10], own.at[2])
-    out_sum = Scatter(CUT_OUT, out_parts, out_recv1, out_mid, out_recv2, hmine.at[pl.ds(SHARE, sum(CUT_OUT))], *sems[11])
+    head_all = Spread(hmine, agh, WAYS_HEAD, *sems[10], own.at[2])
+    out_all = Spread(out_share, agw, WAYS_OUT, *sems[12], own.at[3])
+    out_sum = Scatter(CUT_OUT, out_parts, out_recv1, out_mid, out_recv2, out_share, *sems[11])
     row = lax.axis_index("rows")
 
     def line(ref):
@@ -654,19 +647,22 @@
             ready("bv")
             y = y + line(bv)
         low = jnp.transpose(y).astype(bf16).reshape(H, HS, TOK)
-        if t < 2:
-            qkt[:, t * HS : (t + 1) * HS, :] = low
-        else:
-            vals[...] = low
-        if t == 0:
-            pl.semaphore_wait(bar, count)
-            moved = [Exchange(qkt, rqk, asend.at[0], arecv.at[0]).all()]
-    moved.append(Exchange(vals, rv, asend.at[1], arecv.at[1]).all())
+        qkvt[:, t * HS : (t + 1) * HS, :] = low
+    pl.semaphore_wait(bar, count)
+    moved = Exchange(qkvt, rqk, asend.at[0], arecv.at[0]).all()
+    load("out", wout_h, wout)
+    for name, src, dst in (
+        ("bout", bout_h, bout), ("ln2g", ln2g_h, ln2g), ("ln2b", ln2b_h, ln2b),
+        ("bup", bup_h, bup), ("bdown", bdown_h, bdown),
+    ):
+        load(name, src, dst)
+    load("up", wup_h, wup)
+    load("down", wdown_h, wdown)
     ready("dy", "offs")
     dya[row] = dy_ref[...]
     dy_rows.step()
-    for copy in moved:
-        copy.wait()
+    moved.wait()
+    rv = rqk.at[:, pl.ds(2 * HS, HS)]
     gather.step()
 
     attended = Exchange(atts, ratt, asend.at[2], arecv.at[2])
@@ -774,16 +770,30 @@
             early.step()
         elif i == 6:
             part_out()
-        elif i == 4:
+        elif i == 5:
             grads_down()
         elif i == 1:
             down_sum.step()
 
     attend_backward(offs, rqk, rv, kn, kt, vn, qn, don, rda, ot, lse, dqkv, dk, dv, between)
+    gather.step()
+    spread = jnp.concatenate([dqkv[k] for k in range(NB)], axis=1)
+
+    def part_head(slot, half):
+        res = dot(spread, hall[half].reshape(SEQ, 384)).astype(bf16)
+        for u in range(3):
+            hpart[slot, u * 144 : (u + 1) * 144, :] = res[:, u * TOK : (u + 1) * TOK]
+        hpart[slot, 432:HEAD_ROWS, :] = jnp.zeros((HEAD_ROWS - 432, TOK), bf16)
+
+    part_head(1, other)
+    heads.step()
+    part_head(0, core)
     h2_rows.step()
+    heads.step()
     grads_up()
     back.wait()
-
+    down_sum.step()
+    down_all.step()
     dh1t = None
     ones = jnp.ones((8, TOK), bf16)
     for t in range(3):
@@ -798,56 +808,46 @@
     vecl[LN1G : LN1G + 1, :] = over_tokens(dh1 * n)
     vecl[LN1B : LN1B + 1, :] = over_tokens(dh1)
     vecl[4:8, :] = jnp.zeros((4, D), f32)
-    gather.step()
-    spread = jnp.concatenate([dqkv[k] for k in range(NB)], axis=1)
-
-    def part_head(slot, half):
-        res = dot(spread, hall[half].reshape(SEQ, 384)).astype(bf16)
-        for u in range(3):
-            hpart[slot, u * 144 : (u + 1) * 144, :] = res[:, u * TOK : (u + 1) * TOK]
-        hpart[slot, 432:HEAD_ROWS, :] = jnp.zeros((HEAD_ROWS - 432, TOK), bf16)
-
-    part_head(1, other)
-    heads.step()
-    down_sum.step()
-    down_all.step()
-    part_head(0, core)
     early.step()
     late.step()
     grads_out()
-    heads.step()
     up_sum.step()
     down_all.step()
     late.step()
-    ig_ref[...] = (gres[...] + norm_back(dh1, n, rs1[...], line(ln1g))).astype(bf16)
-    store(ig_ref, ig_h)
     out_sum.step()
     heads.step()
-    early.step()
+    head_all.step()
     up_sum.step()
-    up_all.step()
-    down_all.step()
-    late.step()
-    out_sum.step()
-    head_all.step()
     up_all.step()
     early.step()
     down_all.step()
+    up_all.step()
+    head_all.step()
+    ig_ref[...] = (gres[...] + norm_back(dh1, n, rs1[...], line(ln1g))).astype(bf16)
+    store(ig_ref, ig_h)
+    down_all.step()
+    out_sum.step()
+    out_all.step()
+    up_all.step()
+    out_all.step()
     late.step()
     head_all.step()
+    down_all.step()
+    out_all.step()
+    up_all.step()
+    head_all.step()
+    late.step()
+    early.step()
     late.step()
     early.step()
     vecs[0] = vbuf[1]
     vecs[1] = lbuf[1]
     store(vecs, vecs_h)
+    out_all.step()
     up_all.step()
     head_all.step()
-    up_all.step()
-    head_all.step()
-    down_all.step()
-    up_all.step()
-    head_all.step()
-    for item in (down_all, up_all, head_all):
+    out_all.step()
+    for item in (down_all, up_all, head_all, out_all):
         item.step()
     for item in (down_sum, up_sum, out_sum):
         item.done()
@@ -872,17 +872,18 @@
             v((TOK, D), bf16),
             v((2, 4, 4, 4, sum(CUT_DOWN), TOK), bf16),
             v((2, 4, 4, 4, sum(CUT_UP), TOK), bf16),
-            v((2, 4, 4, 4, ROWS_LAST, TOK), bf16),
+            v((2, 4, 4, 4, SHARE, TOK), bf16),
+            v((2, 4, 4, 4, sum(CUT_OUT), TOK), bf16),
             v((2, VROWS, D), f32),
         ),
         in_specs=[HBM] * 16,
-        out_specs=(ANY,) * 6,
+        out_specs=(ANY,) * 7,
         scratch_shapes=[
             pltpu.SMEM((1, 8), jnp.int32), v((TOK, D), bf16), v((TOK, D), bf16),
             *[v((FF if k == 7 else D,), bf16) for k in range(9)],
             v((TOK, D), bf16), v((TOK, D), bf16), v((2, VROWS, D), f32),
             v((D, 3 * D), bf16), v((D, D), bf16), v((D, FF), bf16), v((FF, D), bf16), dma((20,)),
-            v((NB, 96, TOK), bf16), v((NB, HS, TOK), bf16), v((NB, 96, TOK), bf16), v((NB, HS, TOK), bf16),
+            v((NB, 144, TOK), bf16), v((NB, 144, TOK), bf16),
             v((SEQ, HS), bf16), v((HS, SEQ), bf16),
             v((HS, SEQ), f32), v((1, SEQ), f32), v((NB, HS, TOK), bf16), v((NB, HS, TOK), bf16),
             v((2, 4, 4, TOK, 384), bf16), v((TOK, D), f32), v((TOK, 1), f32),
@@ -897,16 +898,16 @@
             v((2, VROWS, D), f32), v((4, 4, VROWS, D), f32), dma((4,)), dma((4,)),
             v((2, VROWS, D), f32), v((4, 4, VROWS, D), f32), dma((4,)), dma((4,)), dma((3,)),
             dma((3,)), dma((3,)), v((2, HEAD_ROWS, TOK), bf16), v((HEAD_ROWS, TOK), bf16),
-            v((HEAD_ROWS, TOK), bf16), v((3, SHARE, TOK), bf16), v((ROWS_LAST, TOK), bf16),
+            v((HEAD_ROWS, TOK), bf16), v((3, SHARE, TOK), bf16), v((SHARE, TOK), bf16),
             v((4, 576, TOK), bf16), v((3, 576, TOK), bf16),
-            *[dma((n,)) for n in (2, 3, 3, 1, 1, 1, 4, 4, 5, 5, 5, 4) for _ in range(2)], dma((3,)),
+            *[dma((n,)) for n in (2, 3, 3, 1, 1, 1, 4, 4, 5, 5, 5, 4, 5) for _ in range(2)], dma((4,)),
             *[
                 v(lead + (cut, TOK), bf16)
                 for cuts in (CUT_DOWN, CUT_UP, CUT_OUT)
                 for lead in ((4, 4), (3, 4), (4,), (3,))
                 for cut in cuts
             ],
-            v((sum(CUT_DOWN), TOK), bf16), v((sum(CUT_UP), TOK), bf16),
+            v((sum(CUT_DOWN), TOK), bf16), v((sum(CUT_UP), TOK), bf16), v((sum(CUT_OUT), TOK), bf16),
         ],
         compiler_params=pltpu.CompilerParams(
             collective_id=1, has_side_effects=True, vmem_limit_bytes=43 * 2**20
@@ -914,7 +915,7 @@
     )(*[pltpu.with_memory_space_constraint(a, pltpu.HBM) for a in (offsets, x, dy, *vectors, *weights)])
 
 
-def widen_kernel(ag0, ag1, agh, vecs, done_h, ig_h, wqkv, wout, wup, wdown, out_h, grad_h, *rest):
+def widen_kernel(ag0, ag1, agh, agw, vecs, done_h, ig_h, wqkv, wout, wup, wdown, out_h, grad_h, *rest):
     small_h, small = rest[:9], rest[9:18]
     down_out, up_out, out_out, wideb, vsem, ssem, osem = rest[18:]
     passed = [
@@ -978,7 +979,7 @@
             widen(ag1, CUT_UP, 0, k, t * D, D, up_out.at[k % 3], t)
         up_store[k].start()
         for t in range(6):
-            widen(agh, CUT_OUT, SHARE, k, t * 96, 96, out_out.at[k % 3], t)
+            widen(agw, CUT_OUT, 0, k, t * 96, 96, out_out.at[k % 3], t)
         out_store[k].start()
         if k < 6:
             if k >= 3:
@@ -1020,7 +1021,7 @@
             shape((D, 3 * D), f32), shape((D, D), f32), shape((D, FF), f32), shape((FF, D), f32),
             shape((TOK, D), bf16), shape((TOK, D), bf16),
         ) + tuple(shape((FF if k == 7 else D,), f32) for k in range(9)),
-        in_specs=[VMEM] * 4 + [ANY] * 2,
+        in_specs=[VMEM] * 5 + [ANY] * 2,
         out_specs=(ANY,) * 15,
         scratch_shapes=[
             *[v((FF if k == 7 else D,), f32) for k in range(9)],
@@ -1035,12 +1036,12 @@
     block_input, offsets, ln1_gain, ln1_bias, w_qkv, bias_query, bias_value, w_out, bias_out,
     ln2_gain, ln2_bias, w_up, bias_up, w_down, bias_down, cotangent,
 ):
-    out, ig, ag0, ag1, agh, vecs = call_block(
+    out, ig, ag0, ag1, agh, agw, vecs = call_block(
         offsets, block_input.reshape(TOK, D), cotangent.reshape(TOK, D),
         (ln1_gain, ln1_bias, bias_query, bias_value, bias_out, ln2_gain, ln2_bias, bias_up, bias_down),
         (w_qkv, w_out, w_up, w_down),
     )
-    wide = call_widen(ag0, ag1, agh, vecs, out, ig)
+    wide = call_widen(ag0, ag1, agh, agw, vecs, out, ig)
     g_qkv, g_out, g_up, g_down, out, ig = wide[:6]
     s = wide[6:]
     return (

time: 121 us -> 119 us (0.983)
  Pallas kernels: 121 us -> 118 us
    pallas_call x1, Pallas kernels: 111 us -> 108 us  [call_block(): pl.pallas_call(block_kernel, out_shape=(v((TOK, D), bf16), v((TOK, D), bf...]
where the time goes in v5:
time: 119 us
  Pallas kernels  118 us (99%)
    pallas_call x1, Pallas kernels, call_block(): pl.pallas_call(block_kernel, out_shape=(v((TOK, D), bf16), v((TOK, D), bf...  108 us
    pallas_call x1, Pallas kernels, call_widen(): pl.pallas_call(widen_kernel, out_shape=(shape((D, 3 * D), f32), shape((D,...  9.93 us

profile of v5, /device:TPU:1, one launch (start us, length us, event | category | flops | bytes accessed | tf_op | source)
XLA Modules:
  0.0 119.2 jit_solution(12086261856054760858)
XLA Ops:
  0.7 108.4 %shard_map.271 = (bf16[128,768]{1,0:T(8,128)(2,1)S(1)}, bf16[128,768]{1,0:T(8,128)(2,1)S(1)}, bf16[2,4,4,4,144,128]{5,4,3,2,1,0:T(8,128)(2,1)S(1)}, bf16[2,4,4,4...) custom-call(s32[1,8]{1,0:T(1,128)} %offs_h.1, ...), custom_call_target="tpu_custom_call" | custom-call | tf_op jit(solution)/shard_map/pallas_call | solution.py:868
  109.0 9.9 %shard_map.272 = (f32[768,2304]{1,0:T(8,128)}, f32[768,768]{1,0:T(8,128)}, f32[768,3072]{1,0:T(8,128)}, f32[3072,768]{1,0:T(8,128)}, bf16[128,768]{1,0:T(8,128)(...) custom-call(bf16[2,4,4,4,144,128]{5,4,3,2,1,0:T(8,128)(2,1)S(1)} %ge, ...), custom_call_target="tpu_custom_call" | custom-call | tf_op jit(solution)/shard_map/pallas_call | solution.py:1018

commit v6 on v5

--- a/solution.py
+++ b/solution.py
@@ -127,9 +127,11 @@
     return jnp.concatenate([ref[2 * i, lo:hi, :], ref[2 * i + 1, lo:hi, :]], axis=1)
 
 
-def attend_forward(offs_ref, qk, vals, kn, vt, ot, lse, atts, after):
+def attend_forward(offs_ref, qk, vals, kn, vt, ot, lse, atts, values_here, after):
     for s in range(NB):
         kn[s * TOK : (s + 1) * TOK, :] = turned(qk[s, 48:96, :])
+    values_here()
+    for s in range(NB):
         vt[:, s * TOK : (s + 1) * TOK] = vals[s]
     for i in range(SEQ // QB):
         q0 = i * QB
@@ -551,7 +553,7 @@
     offs, x_ref, dy_ref, ln1g, ln1b, bq, bv, bout, ln2g, ln2b, bup, bdown,
     out_ref, ig_ref, vecs,
     wqkv, wout, wup, wdown, wsem,
-    qkvt, rqk, kn, vt, ot, lse, atts, ratt,
+    qkt, vals, rqk, rv, kn, vt, ot, lse, atts, ratt,
     hall, n1, rs1, h2ta, dya, actt, acta, gp, gpa, gb, gbs, attts, gres,
     gattt, rda, kt, vn, qn, don, dk, dv, dqkv, rdq,
     asend, arecv, ssend, srecv,
@@ -647,9 +649,14 @@
             ready("bv")
             y = y + line(bv)
         low = jnp.transpose(y).astype(bf16).reshape(H, HS, TOK)
-        qkvt[:, t * HS : (t + 1) * HS, :] = low
-    pl.semaphore_wait(bar, count)
-    moved = Exchange(qkvt, rqk, asend.at[0], arecv.at[0]).all()
+        if t < 2:
+            qkt[:, t * HS : (t + 1) * HS, :] = low
+        else:
+            vals[...] = low
+        if t == 0:
+            pl.semaphore_wait(bar, count)
+            moved = [Exchange(qkt, rqk, asend.at[0], arecv.at[0]).all()]
+    moved.append(Exchange(vals, rv, asend.at[1], arecv.at[1]).all())
     load("out", wout_h, wout)
     for name, src, dst in (
         ("bout", bout_h, bout), ("ln2g", ln2g_h, ln2g), ("ln2b", ln2b_h, ln2b),
@@ -661,14 +668,13 @@
     ready("dy", "offs")
     dya[row] = dy_ref[...]
     dy_rows.step()
-    moved.wait()
-    rv = rqk.at[:, pl.ds(2 * HS, HS)]
+    moved[0].wait()
     gather.step()
 
     attended = Exchange(atts, ratt, asend.at[2], arecv.at[2])
     attend_forward(
         offs, rqk, rv, kn, vt, ot, lse, atts,
-        attended.one,
+        moved[1].wait, attended.one,
     )
     ready("out", "bout", "ln2g", "ln2b", "bup", "bdown", "up", "down")
     gather.step()
@@ -883,7 +889,7 @@
             *[v((FF if k == 7 else D,), bf16) for k in range(9)],
             v((TOK, D), bf16), v((TOK, D), bf16), v((2, VROWS, D), f32),
             v((D, 3 * D), bf16), v((D, D), bf16), v((D, FF), bf16), v((FF, D), bf16), dma((20,)),
-            v((NB, 144, TOK), bf16), v((NB, 144, TOK), bf16),
+            v((NB, 96, TOK), bf16), v((NB, HS, TOK), bf16), v((NB, 96, TOK), bf16), v((NB, HS, TOK), bf16),
             v((SEQ, HS), bf16), v((HS, SEQ), bf16),
             v((HS, SEQ), f32), v((1, SEQ), f32), v((NB, HS, TOK), bf16), v((NB, HS, TOK), bf16),
             v((2, 4, 4, TOK, 384), bf16), v((TOK, D), f32), v((TOK, 1), f32),

time: 119 us -> 117 us (0.983)
  Pallas kernels: 118 us -> 116 us
    pallas_call x1, Pallas kernels: 108 us -> 106 us  [call_block(): pl.pallas_call(block_kernel, out_shape=(v((TOK, D), bf16), v((TOK, D), bf...]
where the time goes in v6:
time: 117 us
  Pallas kernels  116 us (99%)
    pallas_call x1, Pallas kernels, call_block(): pl.pallas_call(block_kernel, out_shape=(v((TOK, D), bf16), v((TOK, D), bf...  106 us
    pallas_call x1, Pallas kernels, call_widen(): pl.pallas_call(widen_kernel, out_shape=(shape((D, 3 * D), f32), shape((D,...  9.93 us

profile of v6, /device:TPU:1, one launch (start us, length us, event | category | flops | bytes accessed | tf_op | source)
XLA Modules:
  0.0 116.9 jit_solution(6995761229468860070)
XLA Ops:
  0.7 106.2 %shard_map.271 = (bf16[128,768]{1,0:T(8,128)(2,1)S(1)}, bf16[128,768]{1,0:T(8,128)(2,1)S(1)}, bf16[2,4,4,4,144,128]{5,4,3,2,1,0:T(8,128)(2,1)S(1)}, bf16[2,4,4,4...) custom-call(s32[1,8]{1,0:T(1,128)} %offs_h.1, ...), custom_call_target="tpu_custom_call" | custom-call | tf_op jit(solution)/shard_map/pallas_call | solution.py:874
  106.8 9.9 %shard_map.272 = (f32[768,2304]{1,0:T(8,128)}, f32[768,768]{1,0:T(8,128)}, f32[768,3072]{1,0:T(8,128)}, f32[3072,768]{1,0:T(8,128)}, bf16[128,768]{1,0:T(8,128)(...) custom-call(bf16[2,4,4,4,144,128]{5,4,3,2,1,0:T(8,128)(2,1)S(1)} %ge, ...), custom_call_target="tpu_custom_call" | custom-call | tf_op jit(solution)/shard_map/pallas_call | solution.py:1024

commit v7 on v6

--- a/solution.py
+++ b/solution.py
@@ -302,9 +302,9 @@
 
 
 class Spread(Steps):
-    def __init__(self, share, ag, ways, send, recv, own):
+    def __init__(self, share, ag, ways, send, recv, own, at_once=False):
         super().__init__(send, recv)
-        self.share, self.ag, self.ways, self.own = share, ag, ways, own
+        self.share, self.ag, self.ways, self.own, self.at_once = share, ag, ways, own, at_once
 
     def spot(self, lo, size, whole, **at):
         core = lax.rem(lax.axis_index("rows"), 2)
@@ -312,7 +312,8 @@
         return self.ag.at[(core, *index, pl.ds(lo, size))]
 
     def pass_on(self, spot):
-        self.go(4, spot, spot, sibling())
+        if not self.at_once:
+            self.go(4, spot, spot, sibling())
 
     def run(self, k):
         ag = self.ag
@@ -356,6 +357,9 @@
         elif k == 3:
             self.expect(3, ag.at[0, 0])
         elif k == 4:
+            if self.at_once:
+                spot = ag.at[lax.rem(lax.axis_index("rows"), 2)]
+                self.go(4, spot, spot, sibling())
             self.expect(4, ag.at[0])
         else:
             self.done()
@@ -568,6 +572,7 @@
     up_parts, up_recv1, up_mid, up_recv2 = [rest[8 + 2 * k : 10 + 2 * k] for k in range(4)]
     out_parts, out_recv1, out_mid, out_recv2 = [rest[16 + 2 * k : 18 + 2 * k] for k in range(4)]
     down_share, up_share, out_share = rest[24:]
+    bar, count = greet()
     loads = {}
 
     def load(name, src, dst):
@@ -596,7 +601,6 @@
         copy.start()
         stores.append(copy)
 
-    bar, count = greet()
     vecg = vbuf.at[0]
     vecl = lbuf.at[0]
     early = Vectors(vbuf, vrecv, vsend, vrsem)
@@ -610,7 +614,7 @@
     quarters = Quarters(wop, wor, *sems[5])
     down_sum = Scatter(CUT_DOWN, down_parts, down_recv1, down_mid, down_recv2, down_share, *sems[6])
     up_sum = Scatter(CUT_UP, up_parts, up_recv1, up_mid, up_recv2, up_share, *sems[7])
-    down_all = Spread(down_share, ag0, WAYS_DOWN, *sems[8], own.at[0])
+    down_all = Spread(down_share, ag0, WAYS_DOWN, *sems[8], own.at[0], True)
     up_all = Spread(up_share, ag1, WAYS_UP, *sems[9], own.at[1])
     head_all = Spread(hmine, agh, WAYS_HEAD, *sems[10], own.at[2])
     out_all = Spread(out_share, agw, WAYS_OUT, *sems[12], own.at[3])

time: 117 us -> 117 us (level)
  no operation moved by 1% of the time
where the time goes in v7:
time: 117 us
  Pallas kernels  116 us (99%)
    pallas_call x1, Pallas kernels, call_block(): pl.pallas_call(block_kernel, out_shape=(v((TOK, D), bf16), v((TOK, D), bf...  107 us
    pallas_call x1, Pallas kernels, call_widen(): pl.pallas_call(widen_kernel, out_shape=(shape((D, 3 * D), f32), shape((D,...  9.93 us

profile of v7, /device:TPU:1, one launch (start us, length us, event | category | flops | bytes accessed | tf_op | source)
XLA Modules:
  0.0 117.3 jit_solution(4838093625702056303)
XLA Ops:
  0.7 106.6 %shard_map.271 = (bf16[128,768]{1,0:T(8,128)(2,1)S(1)}, bf16[128,768]{1,0:T(8,128)(2,1)S(1)}, bf16[2,4,4,4,144,128]{5,4,3,2,1,0:T(8,128)(2,1)S(1)}, bf16[2,4,4,4...) custom-call(s32[1,8]{1,0:T(1,128)} %offs_h.1, ...), custom_call_target="tpu_custom_call" | custom-call | tf_op jit(solution)/shard_map/pallas_call | solution.py:878
  107.2 9.9 %shard_map.272 = (f32[768,2304]{1,0:T(8,128)}, f32[768,768]{1,0:T(8,128)}, f32[768,3072]{1,0:T(8,128)}, f32[3072,768]{1,0:T(8,128)}, bf16[128,768]{1,0:T(8,128)(...) custom-call(bf16[2,4,4,4,144,128]{5,4,3,2,1,0:T(8,128)(2,1)S(1)} %ge, ...), custom_call_target="tpu_custom_call" | custom-call | tf_op jit(solution)/shard_map/pallas_call | solution.py:1028
